TPU v7x, 128 devices: a whole 4x4x4 slice. The times are simulated.
128 devices in a mesh: pipe: 4 (over z_lo, core), expert: 32 (over z_hi, x, y).
Axes of the slice: x: 4, y: 4, z: 4 (z_hi: 2, z_lo: 2; z = z_hi * 2 + z_lo), core: 2. Of those that a mesh axis runs over, the one named last changes fastest.
Arguments:
- act_fwd: bfloat16 [4, 2048, 3584], P('pipe', 'expert'), may hold values from -40 to 40
- routes_fwd: int32 [4, 2048, 8], P('pipe', 'expert'), may hold values from 0 to 31, all different within a row; in each aligned block of 64 rows (0 to 63, 64 to 127, ..., all dimensions but the last counted through in order) at most 24 rows name the same one
- mix_fwd: float32 [4, 2048, 8], P('pipe', 'expert'), may hold values from 0.2 to 0.8
- cot_bwd: bfloat16 [4, 2048, 3584], P('pipe', 'expert'), may hold values from -6 to 6
- saved_bwd: bfloat16 [4, 2048, 3584], P('pipe', 'expert'), may hold values from -40 to 40
- routes_bwd: int32 [4, 2048, 8], P('pipe', 'expert'), may hold values from 0 to 31, all different within a row; in each aligned block of 64 rows (0 to 63, 64 to 127, ..., all dimensions but the last counted through in order) at most 24 rows name the same one
- mix_bwd: float32 [4, 2048, 8], P('pipe', 'expert'), may hold values from 0.2 to 0.8
- norm_gain: float32 [4, 3584], P('pipe'), may hold values from 0.5 to 1.5
- w_up: bfloat16 [4, 32, 3584, 1024], P('pipe', 'expert'), may hold values from -0.09375 to 0.09375
- w_down: bfloat16 [4, 32, 1024, 3584], P('pipe', 'expert'), may hold values from -0.1875 to 0.1875
Outputs:
- next_fwd: bfloat16 [4, 2048, 3584], P('pipe', 'expert')
- next_bwd: bfloat16 [4, 2048, 3584], P('pipe', 'expert')
Inputs may be any that keep to these rules, and one draw needn't show every extreme that they name: `routes_fwd`: within each section, in each block of 64 consecutive tokens (the tokens of one device) no expert is named by more than 24 tokens, a bound that some block reaches; a token names 8 different experts. `routes_bwd`: as for routes_fwd.
All inputs are finite; a program needn't handle non-finite values.
Results may differ from a plain program's by a relative error of at most 0.006.
Values may be sent and summed in bfloat16 or wider, within the bound.
A program may use at most 128 MiB of HBM per device.

v0:
```python
import jax
import jax.numpy as jnp
from jax import lax
from jax.sharding import PartitionSpec as P


def from_behind(shard, axis, by):
    size = lax.axis_size(axis)
    return lax.ppermute(shard, axis, [(i, (i + by) % size) for i in range(size)])


def normed(values, gain):
    wide = values.astype(jnp.float32)
    recip = lax.rsqrt(jnp.mean(wide * wide, axis=-1, keepdims=True) + 1e-06)
    scaled = wide * recip
    return (scaled, recip, (scaled * gain).astype(jnp.bfloat16))


def slot_index(routes, experts, room):
    targets = routes.reshape(-1)
    one_hot = (targets[:, None] == jnp.arange(experts, dtype=jnp.int32)[None, :]).astype(jnp.int32)
    before = jnp.cumsum(one_hot, axis=0) - one_hot
    return targets * room + jnp.sum(before * one_hot, axis=1)


def packed(token_rows, slots, experts, room):
    width = token_rows.shape[-1]
    buffer = jnp.zeros((experts * room, width), jnp.bfloat16).at[slots].set(token_rows)
    return buffer.reshape(experts, room, width)


def expert_forward(received, up_w, down_w):
    token_rows = received.reshape(-1, received.shape[-1])
    pre_act = jnp.dot(token_rows, up_w, preferred_element_type=jnp.float32)
    hidden = jax.nn.silu(pre_act).astype(jnp.bfloat16)
    result = jnp.dot(hidden, down_w, preferred_element_type=jnp.float32).astype(jnp.bfloat16)
    return result.reshape(received.shape)


def expert_backward(received_u, received_g, up_w, down_w):
    token_rows = received_u.reshape(-1, received_u.shape[-1])
    grad_rows = received_g.reshape(-1, received_g.shape[-1])
    pre_act = jnp.dot(token_rows, up_w, preferred_element_type=jnp.float32)
    sigma = jax.nn.sigmoid(pre_act)
    grad_hidden = lax.dot_general(
        grad_rows, down_w, (((1,), (1,)), ((), ())), preferred_element_type=jnp.float32
    )
    grad_pre = (grad_hidden * sigma * (1.0 + pre_act * (1.0 - sigma))).astype(jnp.bfloat16)
    result = lax.dot_general(
        grad_pre, up_w, (((1,), (1,)), ((), ())), preferred_element_type=jnp.float32
    )
    return result.astype(jnp.bfloat16).reshape(received_u.shape)


def per_device(
    act_fwd, routes_fwd, mix_fwd, cot_bwd, saved_bwd, routes_bwd, mix_bwd, norm_gain, w_up, w_down
):
    rows_here = act_fwd.shape[1]
    width = act_fwd.shape[2]
    top_count = routes_fwd.shape[2]
    experts = lax.axis_size("expert") * w_up.shape[1]
    room = min(rows_here, 3 * rows_here * top_count // (2 * experts))
    gain = norm_gain[0]
    up_w = w_up[0, 0]
    down_w = w_down[0, 0]
    act = act_fwd[0]
    scaled_f, recip_f, normed_f = normed(act, gain)
    slots_f = slot_index(routes_fwd[0], experts, room)
    buffer_f = packed(jnp.repeat(normed_f, top_count, axis=0), slots_f, experts, room)
    cot = cot_bwd[0]
    scaled_b, recip_b, normed_b = normed(saved_bwd[0], gain)
    slots_b = slot_index(routes_bwd[0], experts, room)
    weighted = (mix_bwd[0][:, :, None] * cot.astype(jnp.float32)[:, None, :]).astype(jnp.bfloat16)
    buffer_u = packed(jnp.repeat(normed_b, top_count, axis=0), slots_b, experts, room)
    buffer_g = packed(weighted.reshape(-1, width), slots_b, experts, room)
    result_f = expert_forward(
        lax.all_to_all(buffer_f, "expert", split_axis=0, concat_axis=0, tiled=True), up_w, down_w
    )
    back_f = lax.all_to_all(result_f, "expert", split_axis=0, concat_axis=0, tiled=True)
    result_b = expert_backward(
        lax.all_to_all(buffer_u, "expert", split_axis=0, concat_axis=0, tiled=True),
        lax.all_to_all(buffer_g, "expert", split_axis=0, concat_axis=0, tiled=True),
        up_w,
        down_w,
    )
    back_b = lax.all_to_all(result_b, "expert", split_axis=0, concat_axis=0, tiled=True)
    picked_f = (
        back_f.reshape(experts * room, width)[slots_f]
        .reshape(rows_here, top_count, width)
        .astype(jnp.float32)
    )
    output = (act.astype(jnp.float32) + jnp.sum(mix_fwd[0][:, :, None] * picked_f, axis=1)).astype(
        jnp.bfloat16
    )
    picked_b = (
        back_b.reshape(experts * room, width)[slots_b]
        .reshape(rows_here, top_count, width)
        .astype(jnp.float32)
    )
    grad_norm = jnp.sum(picked_b, axis=1) * gain
    grad_x = recip_b * (
        grad_norm - scaled_b * jnp.mean(grad_norm * scaled_b, axis=-1, keepdims=True)
    )
    grad = (cot.astype(jnp.float32) + grad_x).astype(jnp.bfloat16)
    next_fwd = from_behind(output[None], "pipe", 1)
    next_bwd = from_behind(grad[None], "pipe", -1)
    return (next_fwd, next_bwd)


def solution(mesh):
    return jax.shard_map(
        per_device,
        mesh=mesh,
        in_specs=(
            P("pipe", "expert", None),
            P("pipe", "expert", None),
            P("pipe", "expert", None),
            P("pipe", "expert", None),
            P("pipe", "expert", None),
            P("pipe", "expert", None),
            P("pipe", "expert", None),
            P("pipe", None),
            P("pipe", "expert", None, None),
            P("pipe", "expert", None, None),
        ),
        out_specs=(P("pipe", "expert", None), P("pipe", "expert", None)),
        check_vma=False,
    )
```

profile of v0, /device:TPU:6, one launch (start us, length us, event | category | flops | bytes accessed | tf_op | source)
XLA Modules:
  0.0 518.4 jit_solution(1316918183603880190)
XLA Ops:
  0.6 0.7 broadcast_multiply_fusion
  1.3 0.8 copy.19
  2.5 1.2 reduce-window.16
  3.6 0.2 slice_reduce_fusion
  3.9 1.1 convert_bitcast_fusion.1
  5.0 0.8 copy.22
  6.0 8.9 %scatter_custom_fusion.1 = bf16[768,3584]{1,0:T(8,128)(2,1)} fusion(s32[512]{0:T(512)S(1)} %bitcast.139, f32[64,3584]{1,0:T(8,128)S(1)} %convert_bitcast_fusion.1, f32[512]{0:T(512)S(1)} %mul.170, bf16[]{:T(256)} %constant.9.clone.1), kind=kCustom, calls=%fused_computation.22 | custom fusion | flops 3670016 | bytes 6424578 | tf_op jit(solution)/shard_map/scatter | solution.py:28
  14.8 11.4 %all-to-all-start.2 = ((bf16[32,24,3584]{2,1,0:T(8,128)(2,1)}), bf16[32,24,3584]{2,1,0:T(8,128)(2,1)}, u32[]{:S(2)}, u32[]{:S(2)}) async-start(bf16[32,24,3584]{2,1,0:T(8,128)(2,1)} %bitcast.133), calls=%async_computation.2 | async-start | bytes 11010048 | tf_op jit(solution)/shard_map/all_to_all | solution.py:82
  26.9 8.7 %scatter_custom_fusion.2 = bf16[768,3584]{1,0:T(8,128)(2,1)} fusion(s32[512]{0:T(512)S(1)} %bitcast.140, bf16[]{:T(256)} %constant.9.clone.1, bf16[64,3584]{1,0:T(8,128)(2,1)S(1)} %fusion.46), kind=kCustom, calls=%fused_computation.23 | custom fusion | bytes 5963778 | tf_op jit(solution)/shard_map/scatter | solution.py:28
  35.6 70.9 %all-to-all-done.2 = bf16[32,24,3584]{2,1,0:T(8,128)(2,1)} async-done(((bf16[32,24,3584]{2,1,0:T(8,128)(2,1)}), bf16[32,24,3584]{2,1,0:T(8,128)(2,1)}, u32[]{:S(2)}, u32[]{:S(2)}) %all-to-all-start.2) | async-done | bytes 5505056 | tf_op jit(solution)/shard_map/all_to_all | solution.py:82
  106.5 5.2 %all-to-all-start.3 = ((bf16[32,24,3584]{2,1,0:T(8,128)(2,1)}), bf16[32,24,3584]{2,1,0:T(8,128)(2,1)}, u32[]{:S(2)}, u32[]{:S(2)}) async-start(bf16[32,24,3584]{2,1,0:T(8,128)(2,1)} %bitcast.134), calls=%async_computation.3 | async-start | bytes 11010048 | tf_op jit(solution)/shard_map/all_to_all | solution.py:81
  111.7 10.9 %fusion.2 = f32[768,1024]{1,0:T(8,128)} fusion(bf16[768,3584]{1,0:T(8,128)(2,1)} %bitcast.21, bf16[1,1,1024,3584]{3,2,1,0:T(8,128)(2,1)} %param.19), kind=kOutput, calls=%fused_computation.10 | convolution fusion | flops 5637144576 | bytes 15990784 | tf_op jit(solution)/shard_map/dot_general | solution.py:45
  122.6 63.8 %all-to-all-done.3 = bf16[32,24,3584]{2,1,0:T(8,128)(2,1)} async-done(((bf16[32,24,3584]{2,1,0:T(8,128)(2,1)}), bf16[32,24,3584]{2,1,0:T(8,128)(2,1)}, u32[]{:S(2)}, u32[]{:S(2)}) %all-to-all-start.3) | async-done | bytes 5505056 | tf_op jit(solution)/shard_map/all_to_all | solution.py:81
  186.4 21.6 %fusion.12 = bf16[768,3584]{1,0:T(8,128)(2,1)} fusion(bf16[1,1,3584,1024]{3,2,1,0:T(8,128)(2,1)} %param.18, f32[768,1024]{1,0:T(8,128)} %fusion.2, bf16[768,3584]{1,0:T(8,128)(2,1)} %bitcast.24), kind=kOutput, calls=%fused_computation.20 | convolution fusion | flops 11284119552 | bytes 21495808 | tf_op jit(solution)/shard_map/dot_general | solution.py:49
  208.0 7.9 %all-to-all-start.4 = ((bf16[32,24,3584]{2,1,0:T(8,128)(2,1)}), bf16[32,24,3584]{2,1,0:T(8,128)(2,1)}, u32[]{:S(2)}, u32[]{:S(2)}) async-start(bf16[32,24,3584]{2,1,0:T(8,128)(2,1)} %bitcast.136), calls=%async_computation.4 | async-start | bytes 11010048 | tf_op jit(solution)/shard_map/all_to_all | solution.py:86
  216.4 1.2 reduce-window.14
  218.0 77.9 %all-to-all-done.4 = bf16[32,24,3584]{2,1,0:T(8,128)(2,1)} async-done(((bf16[32,24,3584]{2,1,0:T(8,128)(2,1)}), bf16[32,24,3584]{2,1,0:T(8,128)(2,1)}, u32[]{:S(2)}, u32[]{:S(2)}) %all-to-all-start.4) | async-done | bytes 5505056 | tf_op jit(solution)/shard_map/all_to_all | solution.py:86
  295.9 11.2 %gather_fusion.1 = bf16[512,3584]{1,0:T(8,128)(2,1)} fusion(bf16[768,3584]{1,0:T(8,128)(2,1)} %bitcast.26, s32[1024]{0:T(1024)S(1)} %pad_clamp_fusion), kind=kCustom, calls=%fused_computation.1 | custom fusion | bytes 7342080 | tf_op jit(solution)/shard_map/gather | solution.py:96
  307.0 4.5 convert_reduce_fusion
  311.5 0.3 fusion.47
  311.8 9.2 %scatter_custom_fusion = bf16[768,3584]{1,0:T(8,128)(2,1)} fusion(s32[512]{0:T(512)S(1)} %bitcast.142, bf16[]{:T(256)} %constant.9.clone.1, bf16[64,3584]{1,0:T(8,128)(2,1)S(1)} %get-tuple-element.3), kind=kCustom, calls=%fused_computation.25 | custom fusion | bytes 5963778 | tf_op jit(solution)/shard_map/scatter | solution.py:28
  321.1 69.3 %all_to_all.25 = bf16[32,24,3584]{2,1,0:T(8,128)(2,1)} all-to-all(bf16[32,24,3584]{2,1,0:T(8,128)(2,1)} %bitcast.135), channel_id=1, replica_groups=mesh['pipe'=4,'expert'=32] {'expert'}, dimensions={0} | all-to-all | bytes 11010048 | tf_op jit(solution)/shard_map/all_to_all | solution.py:77
  390.4 19.6 %fusion.15 = bf16[768,3584]{1,0:T(8,128)(2,1)} fusion(bf16[1,1,1024,3584]{3,2,1,0:T(8,128)(2,1)} %param.19, bf16[768,3584]{1,0:T(8,128)(2,1)} %bitcast.138, bf16[1,1,3584,1024]{3,2,1,0:T(8,128)(2,1)} %param.18), kind=kOutput, calls=%fused_computation.21 | convolution fusion | flops 11280973824 | bytes 25690112 | tf_op jit(solution)/shard_map/dot_general | solution.py:36
  409.9 6.7 %all-to-all-start.1 = ((bf16[32,24,3584]{2,1,0:T(8,128)(2,1)}), bf16[32,24,3584]{2,1,0:T(8,128)(2,1)}, u32[]{:S(2)}, u32[]{:S(2)}) async-start(bf16[32,24,3584]{2,1,0:T(8,128)(2,1)} %bitcast.137), calls=%async_computation.1 | async-start | bytes 11010048 | tf_op jit(solution)/shard_map/all_to_all | solution.py:79
  416.8 0.3 fusion.52
  417.1 0.2 collective-permute-start.1
  417.3 75.0 %all-to-all-done.1 = bf16[32,24,3584]{2,1,0:T(8,128)(2,1)} async-done(((bf16[32,24,3584]{2,1,0:T(8,128)(2,1)}), bf16[32,24,3584]{2,1,0:T(8,128)(2,1)}, u32[]{:S(2)}, u32[]{:S(2)}) %all-to-all-start.1) | async-done | bytes 5505056 | tf_op jit(solution)/shard_map/all_to_all | solution.py:79
  492.3 11.2 %gather_fusion = bf16[512,3584]{1,0:T(8,128)(2,1)} fusion(bf16[768,3584]{1,0:T(8,128)(2,1)} %bitcast.11, s32[1024]{0:T(1024)S(1)} %pad_clamp_fusion.1), kind=kCustom, calls=%fused_computation | custom fusion | bytes 7342080 | tf_op jit(solution)/shard_map/gather | solution.py:88
  503.6 5.1 fusion
  508.8 7.9 %collective-permute-done = bf16[1,64,3584]{2,1,0:T(8,128)(2,1)S(1)} collective-permute-done((bf16[1,64,3584]{2,1,0:T(8,128)(2,1)S(1)}, bf16[1,64,3584]{2,1,0:T(8,128)(2,1)S(1)}, u32[]{:S(2)}, u32[]{:S(2)}) %collective-permute-start) | collective-permute-done | bytes 458784 | tf_op jit(solution)/shard_map/ppermute | solution.py:9
  516.7 0.8 copy.29
  517.5 0.8 copy.30
  (46 shorter events, 2.3 us)
Async XLA Ops:
  14.8 11.4 %copy-start.4 = (f32[1,3584]{1,0:T(1,128)S(1)}, f32[1,3584]{1,0:T(1,128)}, u32[]{:S(2)}) copy-start(f32[1,3584]{1,0:T(1,128)} %param.17) | copy-start | bytes 43012
  14.8 11.5 %copy-start = (bf16[1,64,3584]{2,1,0:T(8,128)(2,1)S(1)}, bf16[1,64,3584]{2,1,0:T(8,128)(2,1)}, u32[]{:S(2)}) copy-start(bf16[1,64,3584]{2,1,0:T(8,128)(2,1)} %param.14) | copy-start | bytes 1376260
  14.8 11.7 %copy-start.1 = (bf16[1,64,3584]{2,1,0:T(8,128)(2,1)S(1)}, bf16[1,64,3584]{2,1,0:T(8,128)(2,1)}, u32[]{:S(2)}) copy-start(bf16[1,64,3584]{2,1,0:T(8,128)(2,1)} %param.10) | copy-start | bytes 1376260
  14.8 91.6 %all-to-all-start.2 = ((bf16[32,24,3584]{2,1,0:T(8,128)(2,1)}), bf16[32,24,3584]{2,1,0:T(8,128)(2,1)}, u32[]{:S(2)}, u32[]{:S(2)}) async-start(bf16[32,24,3584]{2,1,0:T(8,128)(2,1)} %bitcast.133), calls=%async_computation.2 | async-start | bytes 11010048 | tf_op jit(solution)/shard_map/all_to_all | solution.py:82
  106.5 79.9 %all-to-all-start.3 = ((bf16[32,24,3584]{2,1,0:T(8,128)(2,1)}), bf16[32,24,3584]{2,1,0:T(8,128)(2,1)}, u32[]{:S(2)}, u32[]{:S(2)}) async-start(bf16[32,24,3584]{2,1,0:T(8,128)(2,1)} %bitcast.134), calls=%async_computation.3 | async-start | bytes 11010048 | tf_op jit(solution)/shard_map/all_to_all | solution.py:81
  208.0 7.9 %copy-start.3 = (s32[1,64,8]{1,2,0:T(8,128)S(1)}, s32[1,64,8]{1,2,0:T(8,128)}, u32[]{:S(2)}) copy-start(s32[1,64,8]{1,2,0:T(8,128)} %param.11) | copy-start | bytes 6148
  208.0 87.9 %all-to-all-start.4 = ((bf16[32,24,3584]{2,1,0:T(8,128)(2,1)}), bf16[32,24,3584]{2,1,0:T(8,128)(2,1)}, u32[]{:S(2)}, u32[]{:S(2)}) async-start(bf16[32,24,3584]{2,1,0:T(8,128)(2,1)} %bitcast.136), calls=%async_computation.4 | async-start | bytes 11010048 | tf_op jit(solution)/shard_map/all_to_all | solution.py:86
  409.9 6.7 %copy-start.5 = (f32[1,64,8]{1,2,0:T(8,128)S(1)}, f32[1,64,8]{1,2,0:T(8,128)}, u32[]{:S(2)}) copy-start(f32[1,64,8]{1,2,0:T(8,128)} %param.12) | copy-start | bytes 6148
  409.9 6.8 %copy-start.2 = (bf16[1,64,3584]{2,1,0:T(8,128)(2,1)S(1)}, bf16[1,64,3584]{2,1,0:T(8,128)(2,1)}, u32[]{:S(2)}) copy-start(bf16[1,64,3584]{2,1,0:T(8,128)(2,1)} %param.13) | copy-start | bytes 1376260
  409.9 82.4 %all-to-all-start.1 = ((bf16[32,24,3584]{2,1,0:T(8,128)(2,1)}), bf16[32,24,3584]{2,1,0:T(8,128)(2,1)}, u32[]{:S(2)}, u32[]{:S(2)}) async-start(bf16[32,24,3584]{2,1,0:T(8,128)(2,1)} %bitcast.137), calls=%async_computation.1 | async-start | bytes 11010048 | tf_op jit(solution)/shard_map/all_to_all | solution.py:79
  417.1 91.7 %collective-permute-start.1 = (bf16[1,64,3584]{2,1,0:T(8,128)(2,1)S(1)}, bf16[1,64,3584]{2,1,0:T(8,128)(2,1)S(1)}, u32[]{:S(2)}, u32[]{:S(2)}) collective-permute-start(bf16[1,64,3584]{2,1,0:T(8,128)(2,1)S(1)} %fusion.52), channel_id=1, source_target_pairs={{0,96},{32,0},{64,32},{96,64},{1,97},{33,1},{65,33},{97,65},{2,98}... | collective-permute-start | bytes 1376264 | tf_op jit(solution)/shard_map/ppermute | solution.py:9
  508.7 8.0 %collective-permute-start = (bf16[1,64,3584]{2,1,0:T(8,128)(2,1)S(1)}, bf16[1,64,3584]{2,1,0:T(8,128)(2,1)S(1)}, u32[]{:S(2)}, u32[]{:S(2)}) collective-permute-start(bf16[1,64,3584]{2,1,0:T(8,128)(2,1)S(1)} %fusion.51), channel_id=1, source_target_pairs={{0,32},{32,64},{64,96},{96,0},{1,33},{33,65},{65,97},{97,1},{2,34}... | collective-permute-start | bytes 1376264 | tf_op jit(solution)/shard_map/ppermute | solution.py:9
where the time goes:
time: 525 us; the launch traced here: 518 us
  waiting for transfers between devices  295 us (56%)
  blocking collectives  69.3 us (13%)
  matrix products  52.1 us (10%)
  local copies, waits for them, and re-layouts  44.9 us (9%)
  starting transfers between devices  31.6 us (6%)
  other arithmetic  24.2 us (5%)
    all_to_all x1, waiting for transfers between devices, per_device(): lax.all_to_all(result_b, 'expert', split_axis=0, concat_axis=0, tiled=True)  77.9 us
    all_to_all x1, waiting for transfers between devices, per_device(): lax.all_to_all(result_f, 'expert', split_axis=0, concat_axis=0, tiled=True)  75 us
    all_to_all x1, waiting for transfers between devices, per_device(): lax.all_to_all(buffer_g, 'expert', split_axis=0, concat_axis=0, tiled=True)  70.9 us
    all_to_all x1, blocking collectives, per_device(): lax.all_to_all(buffer_f, 'expert', split_axis=0, concat_axis=0, tiled=True)  69.3 us
    all_to_all x1, waiting for transfers between devices, per_device(): lax.all_to_all(buffer_u, 'expert', split_axis=0, concat_axis=0, tiled=True)  63.8 us
    dot_general x1, matrix products, expert_backward(): lax.dot_general(grad_pre, up_w, (((1,), (1,)), ((), ())), preferred_eleme...  21.6 us
    dot_general x1, matrix products, expert_forward(): jnp.dot(hidden, down_w, preferred_element_type=jnp.float32)  19.6 us
    scatter x2, local copies, waits for them, and re-layouts, packed(): jnp.zeros((experts * room, width), jnp.bfloat16).at[slots].set(token_rows)  17.9 us
  transfers between devices with their start and end apart: 6, of which 5 were waited for; matrix products, arithmetic and copies ran while one was open for 8% of the time, Pallas kernels for 0%

commit v1 on v0

v1 whole, which is shorter than its diff:
```python
import functools

import jax
import jax.numpy as jnp
from jax import lax
from jax.experimental import pallas as pl
from jax.experimental.pallas import tpu as pltpu
from jax.sharding import PartitionSpec as P

MESH = pl.DeviceIdType.MESH
BF, F32 = jnp.bfloat16, jnp.float32

D, HID, TOP, ROWS, CAP = 3584, 1024, 8, 64, 24
SIDE, DEEP = 4, 2
HALF = D // 2
CH = 256
NCH = HALF // CH
PAIR = DEEP * CAP
LINE = SIDE * PAIR
PT = DEEP * ROWS
NOUT, NRET = 3 * NCH, 2 * NCH
RING = 3


def kernel(
    act, routes_f, mix_f, cot, saved, routes_b, mix_b, gain, wup, wdn,
    next_f, next_b,
    ag, rc, snd, wbu, wbd, ob, zb, zr, xb, xr, gs, acc, gh, hid, sel, scl, cw, tab, ttab, yb, gb,
    a_s, a_r, b_s, b_r, c_s, c_r, e_s, e_r, f_s, f_r, g_s, g_r, w_sem, t_s, t_r, p_s, p_r,
):
    pp, me = lax.axis_index("pipe"), lax.axis_index("expert")
    z, x, y = me // (SIDE * SIDE), (me // SIDE) % SIDE, me % SIDE
    n_pipe = lax.axis_size("pipe")

    def device(dz, dx, dy):
        return (pp, ((z + dz) % DEEP) * SIDE * SIDE + ((x + dx) % SIDE) * SIDE + (y + dy) % SIDE)

    gather_at, trade_at = (x, y), (y, x)
    gather_peer = lambda v, k: device(0, k, 0) if v == 0 else device(0, 0, k)
    trade_peer = lambda v, k: device(0, 0, k) if v == 0 else device(0, k, 0)
    other = device(1, 0, 0)
    ahead, behind = ((pp + 1) % n_pipe, me), ((pp + n_pipe - 1) % n_pipe, me)
    shifts = range(1, SIDE)

    def send(src, dst, s_sem, r_sem, to):
        pltpu.make_async_remote_copy(
            src_ref=src, dst_ref=dst, send_sem=s_sem, recv_sem=r_sem, device_id=to, device_id_type=MESH
        ).start()

    def wait(ref, sem):
        pltpu.make_async_copy(ref, ref, sem).wait()

    barrier = pltpu.get_barrier_semaphore()
    peers = [other, ahead, behind] + [gather_peer(v, k) for v in range(2) for k in shifts]
    for peer in peers:
        pl.semaphore_signal(barrier, inc=1, device_id=peer, device_id_type=MESH)

    lane = lax.broadcasted_iota(jnp.int32, (ROWS, 128), 1)
    expert_of = lane % 32
    is_b = (lane // 32) % 2 == 1
    chosen = jnp.zeros((ROWS, 128), F32)
    weight = jnp.zeros((ROWS, 128), F32)
    for k in range(TOP):
        named = jnp.where(is_b, routes_b[:, k : k + 1], routes_f[:, k : k + 1])
        hit = named == expert_of
        chosen = jnp.where(hit, 1.0, chosen)
        weight = jnp.where(hit, jnp.where(is_b, mix_b[:, k : k + 1], mix_f[:, k : k + 1]), weight)
    earlier = lax.broadcasted_iota(jnp.int32, (ROWS, ROWS), 0) > lax.broadcasted_iota(jnp.int32, (ROWS, ROWS), 1)
    rank = jnp.dot(jnp.where(earlier, 1.0, 0.0).astype(BF), chosen.astype(BF), preferred_element_type=F32)
    slot = jnp.where(chosen > 0.5, rank + (z * CAP + 1).astype(F32), 0.0)
    tab[0, x, z] = jnp.where(lane < 64, slot, weight)

    def spread(array, wide):
        for v in range(2):
            for j in range(NCH):
                lo = v * HALF + j * CH
                ag[array * NCH + j, v, gather_at[v], z] = wide[:, lo : lo + CH].astype(BF)

    def normed(ref):
        wide = ref[...].astype(F32)
        recip = lax.rsqrt(jnp.sum(wide * wide, axis=-1, keepdims=True) * (1.0 / D) + 1e-06)
        return wide * recip, recip

    spread(0, normed(saved)[0] * gain[...])

    def stage_a(n):
        for v in range(2):
            own = ag.at[n, v, gather_at[v], z]
            for k in shifts:
                send(own, own, a_s.at[n], a_r.at[n], gather_peer(v, k))

    def stage_b(n):
        six = ag.at[n, 0, pl.ds(0, 3)]
        wait(six, a_r.at[n])
        for v in range(2):
            part = ag.at[n, v, :, z]
            send(part, part, b_s.at[n], b_r.at[n], other)
        wait(six, a_s.at[n])

    def stage_c(n, array):
        batch = 1 if array < 2 else 0
        ring = n % RING
        wait(ag.at[n, 0], b_r.at[n])

        @pl.when(n >= RING)
        def _():
            wait(snd.at[ring], c_s.at[n - RING])

        def one(q, carry):
            for v in range(2):
                rows = ag[n, v, q].reshape(PT, CH)
                got = jnp.dot(sel[batch, v, q], rows, preferred_element_type=F32)
                if array == 1:
                    got = got * scl[v, q][:, 0:1]
                got = got.astype(BF).reshape(SIDE, PAIR, CH)
                if v == 0:
                    rc[n, 0, q, y] = got[0]
                else:
                    rc[n, 1, x, q] = got[0]
                for d in shifts:
                    snd[ring, v, d - 1, q] = got[d]
            return carry

        lax.fori_loop(0, SIDE, one, 0)
        for k in shifts:
            send(snd.at[ring, 0, k - 1], rc.at[n, 0, :, y], c_s.at[n], c_r.at[n], trade_peer(0, k))
            send(snd.at[ring, 1, k - 1], rc.at[n, 1, x], c_s.at[n], c_r.at[n], trade_peer(1, k))
        wait(ag.at[n, 0], b_s.at[n])

    def fetch(step, down):
        j, ring = (step - 3) % NCH, step % 2
        for v in range(2):
            cols = pl.ds(pl.multiple_of(v * HALF + j * CH, CH), CH)
            if down:
                pltpu.make_async_copy(wdn.at[:, cols], wbd.at[ring, v], w_sem.at[ring]).start()
            else:
                pltpu.make_async_copy(wup.at[cols, :], wbu.at[ring, v], w_sem.at[ring]).start()

    def fetched(step, down):
        ring = step % 2
        wait((wbd if down else wbu).at[ring], w_sem.at[ring])
        return ring

    def next_weights(step, last, down):
        @pl.when(step < last)
        def _():
            fetch(step + 1, down)

        @pl.when(step == last)
        def _():
            fetch(step + 1, not down)

    NT = (((1,), (1,)), ((), ()))

    def stage_d(n, ring, down, total):
        six = rc.at[n, :, pl.ds(0, 3)]
        wait(six, c_r.at[n])

        def one(q, carry):
            out = total[q]
            for v in range(2):
                rows = rc[n, v, q].reshape(LINE, CH)
                if down:
                    out = out + lax.dot_general(rows, wbd[ring, v], NT, preferred_element_type=F32)
                else:
                    out = out + jnp.dot(rows, wbu[ring, v], preferred_element_type=F32)
            total[q] = out
            return carry

        lax.fori_loop(0, SIDE, one, 0)

    def stage_e(r, wring, down):
        ring = r % RING

        @pl.when(r >= RING)
        def _():
            wait(ob.at[ring, :, pl.ds(0, 3)], e_s.at[r - RING])

        def one(q, carry):
            for v in range(2):
                if down:
                    got = jnp.dot(hid[q], wbd[wring, v], preferred_element_type=F32)
                else:
                    got = lax.dot_general(hid[q], wbu[wring, v], NT, preferred_element_type=F32)
                ob[ring, v, q] = got.astype(BF).reshape(SIDE, PAIR, CH)
            return carry

        lax.fori_loop(0, SIDE, one, 0)
        for k in shifts:
            send(ob.at[ring, 0, :, (y + k) % SIDE], rc.at[r, 0, SIDE - k], e_s.at[r], e_r.at[r], trade_peer(0, k))
            send(ob.at[ring, 1, (x + k) % SIDE], rc.at[r, 1, SIDE - k], e_s.at[r], e_r.at[r], trade_peer(1, k))
        for q in range(SIDE):
            rc[r, 0, 0, q] = ob[ring, 0, q, y]
        rc[r, 1, 0] = ob[ring, 1, x]

    def stage_f(r):
        ring = r % RING
        unit = r // NCH
        wait(rc.at[r, :, pl.ds(1, 3)], e_r.at[r])

        @pl.when(r >= RING)
        def _():
            wait(zb.at[ring, :, 0], f_s.at[r - RING])

        def one(q, carry):
            for v in range(2):
                rows = rc[r, v, :, q].reshape(LINE, CH)
                both = jnp.dot(cw[unit, v, q], rows, preferred_element_type=F32)
                part = (both[:PT] + both[PT:]).astype(BF).reshape(DEEP, ROWS, CH)
                for zz in range(DEEP):
                    zb[ring, v, zz, q] = part[zz]
            return carry

        lax.fori_loop(0, SIDE, one, 0)
        for v in range(2):
            send(zb.at[ring, v, 1 - z], zr.at[r, v], f_s.at[r], f_r.at[r], other)

    def stage_g(r):
        ring = r % RING
        wait(zr.at[r], f_r.at[r])

        @pl.when(r >= RING)
        def _():
            wait(xb.at[ring, :, pl.ds(0, 3)], g_s.at[r - RING])

        for v in range(2):
            xb[ring, v] = (zb[ring, v, z].astype(F32) + zr[r, v].astype(F32)).astype(BF)
            for k in shifts:
                send(xb.at[ring, v, (gather_at[v] + k) % SIDE], xr.at[r, v, k - 1], g_s.at[r], g_r.at[r], gather_peer(v, k))

    def summed(r, v):
        out = xb[r % RING, v, gather_at[v]].astype(F32)
        for k in range(SIDE - 1):
            out = out + xr[r, v, k].astype(F32)
        return out

    def stage_h_b(r):
        wait(xr.at[r], g_r.at[r])
        for v in range(2):
            gs[r, v] = summed(r, v)

    def stage_h_f(r):
        wait(xr.at[r], g_r.at[r])
        j = r - NCH
        for v in range(2):
            cols = pl.ds(pl.multiple_of(v * HALF + j * CH, CH), CH)
            yb[j, v] = (act[:, cols].astype(F32) + summed(r, v)).astype(BF)
            send(yb.at[j, v], next_f.at[:, cols], p_s.at[0], p_r.at[0], ahead)

    def finish_b():
        scaled, recip = normed(saved)
        total = jnp.zeros((ROWS, 1), F32)
        parts = []
        for v in range(2):
            for j in range(NCH):
                lo = v * HALF + j * CH
                g_n = gs[j, v] * gain[:, lo : lo + CH]
                gs[j, v] = g_n
                total = total + jnp.sum(g_n * scaled[:, lo : lo + CH], axis=-1, keepdims=True)
        mean = total * (1.0 / D)
        for v in range(2):
            for j in range(NCH):
                lo = v * HALF + j * CH
                g_x = recip * (gs[j, v] - scaled[:, lo : lo + CH] * mean)
                gb[:, lo : lo + CH] = (cot[:, lo : lo + CH].astype(F32) + g_x).astype(BF)
        send(gb, next_b, p_s.at[1], p_r.at[1], behind)

    pl.semaphore_wait(barrier, len(peers))
    send(tab.at[0, x, z], tab.at[0, x, z], t_s.at[0], t_r.at[0], other)
    stage_a(0)
    fetch(3, False)
    spread(1, cot[...])
    stage_a(1)
    wait(tab.at[0, 0, 0], t_r.at[0])
    wait(tab.at[0, 0, 0], t_s.at[0])
    tab[1, y] = tab[0, x]
    for v in range(2):
        for k in shifts:
            send(tab.at[v, gather_at[v]], tab.at[v, gather_at[v]], t_s.at[1], t_r.at[1], gather_peer(v, k))
    stage_b(0)
    spread(2, normed(act)[0] * gain[...])
    stage_b(1)
    stage_a(2)
    acc[...] = jnp.zeros_like(acc)
    gh[...] = jnp.zeros_like(gh)
    six = tab.at[:, pl.ds(0, 3)]
    wait(six, t_r.at[1])
    wait(six, t_s.at[1])

    slot_row = lax.broadcasted_iota(jnp.int32, (PAIR, 128), 0).astype(F32) + 1.0
    token_lane = lax.broadcasted_iota(jnp.int32, (PT, 128), 1)
    w_lane = lax.broadcasted_iota(jnp.int32, (PT, LINE), 1)
    w_slot = (w_lane % PAIR).astype(F32) + 1.0

    def tables(q, carry):
        for v in range(2):
            pair = tab[v, q].reshape(PT, 128)
            ttab[v] = pair.T
            col = [jnp.zeros((PT, LINE), F32) for _ in range(3)]
            for d in range(SIDE):
                if v == 0:
                    e = z * SIDE * SIDE + x * SIDE + (y + d) % SIDE
                else:
                    e = z * SIDE * SIDE + ((x + d) % SIDE) * SIDE + y
                for batch in range(2):
                    hit = ttab[v, pl.ds(e + 32 * batch, 1), :] == slot_row
                    sel[batch, v, q, d * PAIR : (d + 1) * PAIR, :] = jnp.where(hit, 1.0, 0.0).astype(BF)
                    if batch == 1:
                        gate = jnp.where(hit, ttab[v, pl.ds(e + 96, 1), :], 0.0)
                        scl[v, q, d * PAIR : (d + 1) * PAIR, :] = jnp.broadcast_to(
                            jnp.sum(gate, axis=1, keepdims=True), (PAIR, 128)
                        )
                here = w_lane // PAIR == d
                for i, first in enumerate((0, 32, 64)):
                    one = jnp.sum(jnp.where(token_lane == e + first, pair, 0.0), axis=1, keepdims=True)
                    col[i] = jnp.where(here, one, col[i])
            hit_f = jnp.where(col[0] == w_slot, col[2], 0.0)
            high = hit_f.astype(BF)
            cw[1, v, q, :PT] = high
            cw[1, v, q, PT:] = (hit_f - high.astype(F32)).astype(BF)
            cw[0, v, q, :PT] = jnp.where(col[1] == w_slot, 1.0, 0.0).astype(BF)
            cw[0, v, q, PT:] = jnp.zeros((PT, LINE), BF)
        return carry

    lax.fori_loop(0, SIDE, tables, 0)
    stage_c(0, 0)

    s1 = 3 + NCH
    s2 = s1 + NCH
    s3 = s2 + NCH
    s4 = s3 + NCH

    def loop1(s, carry):
        stage_b(s - 1)
        stage_a(s)

        @pl.when(s - 2 < NCH)
        def _():
            stage_c(s - 2, 0)

        @pl.when(s - 2 >= NCH)
        def _():
            stage_c(s - 2, 1)

        next_weights(s, s1 - 1, False)
        stage_d(s - 3, fetched(s, False), False, acc)
        return carry

    lax.fori_loop(3, s1, loop1, 0)

    def loop2(s, carry):
        stage_b(s - 1)
        stage_a(s)

        @pl.when(s - 2 < 2 * NCH)
        def _():
            stage_c(s - 2, 1)

        @pl.when(s - 2 >= 2 * NCH)
        def _():
            stage_c(s - 2, 2)

        next_weights(s, s2 - 1, True)
        stage_d(s - 3, fetched(s, True), True, gh)
        return carry

    lax.fori_loop(s1, s2, loop2, 0)

    def between_b(q, carry):
        p = acc[q]
        sigma = jax.nn.sigmoid(p)
        hid[q] = (gh[q] * sigma * (1.0 + p * (1.0 - sigma))).astype(BF)
        acc[q] = jnp.zeros_like(p)
        return carry

    lax.fori_loop(0, SIDE, between_b, 0)

    def back(s):
        r = s - s2

        @pl.when(r >= 1)
        def _():
            stage_f(r - 1)

        @pl.when(r >= 2)
        def _():
            stage_g(r - 2)

    def loop3(s, carry):
        @pl.when(s - 1 < NOUT)
        def _():
            stage_b(s - 1)

        @pl.when(s < NOUT)
        def _():
            stage_a(s)

        @pl.when(s - 2 < NOUT)
        def _():
            stage_c(s - 2, 2)

        next_weights(s, s3 - 1, False)
        ring = fetched(s, False)
        stage_e(s - s2, ring, False)
        stage_d(s - 3, ring, False, acc)
        back(s)

        @pl.when(s - s2 >= 3)
        def _():
            stage_h_b(s - s2 - 3)

        return carry

    lax.fori_loop(s2, s3, loop3, 0)

    def between_f(q, carry):
        p = acc[q]
        hid[q] = (p * jax.nn.sigmoid(p)).astype(BF)
        return carry

    lax.fori_loop(0, SIDE, between_f, 0)

    def loop4(s, carry):
        @pl.when(s < s4 - 1)
        def _():
            fetch(s + 1, True)

        ring = fetched(s, True)
        stage_e(s - s2, ring, True)
        back(s)
        r = s - s2 - 3

        @pl.when(r < NCH)
        def _():
            stage_h_b(r)

        @pl.when(r >= NCH)
        def _():
            stage_h_f(r)

        @pl.when(r == NCH)
        def _():
            finish_b()

        return carry

    lax.fori_loop(s3, s4, loop4, 0)
    stage_f(NRET - 1)
    stage_g(NRET - 2)
    stage_h_f(NRET - 3)
    stage_g(NRET - 1)
    stage_h_f(NRET - 2)
    stage_h_f(NRET - 1)

    for n in range(NOUT - RING, NOUT):
        wait(snd.at[n % RING], c_s.at[n])
    for r in range(NRET - RING, NRET):
        wait(ob.at[r % RING, :, pl.ds(0, 3)], e_s.at[r])
        wait(zb.at[r % RING, :, 0], f_s.at[r])
        wait(xb.at[r % RING, :, pl.ds(0, 3)], g_s.at[r])
    wait(gb, p_s.at[0])
    wait(gb, p_s.at[1])
    wait(next_f, p_r.at[0])
    wait(next_b, p_r.at[1])


def per_device(
    act_fwd, routes_fwd, mix_fwd, cot_bwd, saved_bwd, routes_bwd, mix_bwd, norm_gain, w_up, w_down
):
    vmem, far = pl.BlockSpec(memory_space=pltpu.VMEM), pl.BlockSpec(memory_space=pl.ANY)
    sems = [pltpu.SemaphoreType.DMA((NOUT,))] * 6 + [pltpu.SemaphoreType.DMA((NRET,))] * 6
    sems += [pltpu.SemaphoreType.DMA((2,))] * 5
    out = jax.ShapeDtypeStruct((ROWS, D), BF)
    next_fwd, next_bwd = pl.pallas_call(
        kernel,
        out_shape=(out, out),
        in_specs=[vmem] * 8 + [far] * 2,
        out_specs=(far, far),
        scratch_shapes=[
            pltpu.VMEM((NOUT, 2, SIDE, DEEP, ROWS, CH), BF),
            pltpu.VMEM((NOUT, 2, SIDE, SIDE, PAIR, CH), BF),
            pltpu.VMEM((RING, 2, SIDE - 1, SIDE, PAIR, CH), BF),
            pltpu.VMEM((2, 2, CH, HID), BF),
            pltpu.VMEM((2, 2, HID, CH), BF),
            pltpu.VMEM((RING, 2, SIDE, SIDE, PAIR, CH), BF),
            pltpu.VMEM((RING, 2, DEEP, SIDE, ROWS, CH), BF),
            pltpu.VMEM((NRET, 2, SIDE, ROWS, CH), BF),
            pltpu.VMEM((RING, 2, SIDE, ROWS, CH), BF),
            pltpu.VMEM((NRET, 2, SIDE - 1, ROWS, CH), BF),
            pltpu.VMEM((NCH, 2, ROWS, CH), F32),
            pltpu.VMEM((SIDE, LINE, HID), F32),
            pltpu.VMEM((SIDE, LINE, HID), F32),
            pltpu.VMEM((SIDE, LINE, HID), BF),
            pltpu.VMEM((2, 2, SIDE, LINE, PT), BF),
            pltpu.VMEM((2, SIDE, LINE, 128), F32),
            pltpu.VMEM((2, 2, SIDE, 2 * PT, LINE), BF),
            pltpu.VMEM((2, SIDE, DEEP, ROWS, 128), F32),
            pltpu.VMEM((2, 128, 128), F32),
            pltpu.VMEM((NCH, 2, ROWS, CH), BF),
            pltpu.VMEM((ROWS, D), BF),
        ]
        + sems,
        compiler_params=pltpu.CompilerParams(
            collective_id=0, has_side_effects=True, vmem_limit_bytes=63 * 2**20
        ),
        cost_estimate=pl.CostEstimate(flops=30 * 10**9, bytes_accessed=40 * 10**6, transcendentals=2 * 10**6),
    )(
        act_fwd[0], routes_fwd[0], mix_fwd[0], cot_bwd[0], saved_bwd[0], routes_bwd[0], mix_bwd[0],
        norm_gain, w_up[0, 0], w_down[0, 0],
    )
    return next_fwd[None], next_bwd[None]


def solution(mesh):
    rows = P("pipe", "expert", None)
    return jax.shard_map(
        per_device,
        mesh=mesh,
        in_specs=(rows,) * 7 + (P("pipe", None),) + (P("pipe", "expert", None, None),) * 2,
        out_specs=(rows, rows),
        check_vma=False,
    )
```

time: 525 us -> 256 us (0.49)
  waiting for transfers between devices: 295 us -> 0 us
  Pallas kernels: 0 us -> 243 us
  blocking collectives: 69.3 us -> 0 us
  matrix products: 52.1 us -> 0 us
  local copies, waits for them, and re-layouts: 44.9 us -> 9.16 us
  starting transfers between devices: 31.6 us -> 0 us
  other arithmetic: 24.2 us -> 0 us
    all_to_all x4 -> x0, waiting for transfers between devices: 288 us -> none  [the longest x1 77.9 us: per_device(): lax.all_to_all(result_b, 'expert', split_axis=0, concat_axis=0, tiled=True)]
    pallas_call x0 -> x1, Pallas kernels: none -> 243 us  [per_device(): pl.pallas_call(kernel, out_shape=(out, out), in_specs=[vmem] * 8 + [far]...]
    all_to_all x1 -> x0, blocking collectives: 69.3 us -> none  [per_device(): lax.all_to_all(buffer_f, 'expert', split_axis=0, concat_axis=0, tiled=True)]
    dot_general x3 -> x0, matrix products: 52.1 us -> none  [the longest x1 21.6 us: expert_backward(): lax.dot_general(grad_pre, up_w, (((1,), (1,)), ((), ())), preferred_eleme...]
    all_to_all x4 -> x0, starting transfers between devices: 31.2 us -> none  [the longest x1 11.4 us: per_device(): lax.all_to_all(buffer_g, 'expert', split_axis=0, concat_axis=0, tiled=True)]
    gather x2 -> x0, local copies, waits for them, and re-layouts: 22.4 us -> none  [the longest x1 11.2 us: per_device(): back_f.reshape(experts * room, width)[slots_f]]
    scatter x2 -> x0, local copies, waits for them, and re-layouts: 17.9 us -> none  [packed(): jnp.zeros((experts * room, width), jnp.bfloat16).at[slots].set(token_rows)]
    reduce_sum x7 -> x0, other arithmetic: 10.5 us -> none  [the longest x1 5.06 us: per_device(): jnp.sum(mix_fwd[0][:, :, None] * picked_f, axis=1)]
  transfers between devices with their start and end apart: 6 -> 0, of which waited for: 5 -> 0; matrix products, arithmetic and copies ran while one was open for 8% -> 0% of each run, Pallas kernels for 0% -> 0%
where the time goes in v1:
time: 256 us; the launch traced here: 253 us
  Pallas kernels  243 us (95%)
  local copies, waits for them, and re-layouts  9.16 us (4%)
    pallas_call x1, Pallas kernels, per_device(): pl.pallas_call(kernel, out_shape=(out, out), in_specs=[vmem] * 8 + [far]...  243 us
    unnamed x6, local copies, waits for them, and re-layouts  9.16 us

profile of v1, /device:TPU:6, one launch (start us, length us, event | category | flops | bytes accessed | tf_op | source)
XLA Modules:
  0.0 252.8 jit_solution(17050932703475215074)
XLA Ops:
  0.6 1.4 copy.12
  2.0 1.4 copy.13
  3.4 1.4 copy.14
  4.8 1.4 copy.15
  6.2 243.0 %shard_map.113 = (bf16[64,3584]{1,0:T(8,128)(2,1)}, bf16[64,3584]{1,0:T(8,128)(2,1)}) custom-call(bf16[64,3584]{1,0:T(8,128)(2,1)} %bitcast.19, s32[64,8]{1,0:T(8,128)} %bitcast.13, f32[64,8]{1,0:T(8,128)} %bitcast.14, bf16[64,3584]{1,0:T(8,128)(2,1)} %bitcast.20, bf16[64,3584]{1,0:T(8,128)(2,1)} %bitcast.21, s32[64,8]{1,0:T(8,128)} %bitcast.15, ...), custom_call_target="tpu_custom_call" | custom-call | flops 30000001024 | bytes 40000000 | tf_op jit(solution)/shard_map/pallas_call | solution.py:474
  249.2 1.8 copy.18
  251.0 1.8 copy.19

commit v2 on v1

--- a/solution.py
+++ b/solution.py
@@ -19,7 +19,9 @@
 LINE = SIDE * PAIR
 PT = DEEP * ROWS
 NOUT, NRET = 3 * NCH, 2 * NCH
-RING = 3
+RING_S, RING_O, RING_Z, RING_X = 3, 4, 4, 8
+AT_A, AT_B, AT_C, AT_D = 0, 2, 4, 6
+AT_F, AT_G, AT_H = AT_D + 2 * NCH + 3, AT_D + 2 * NCH + 6, AT_D + 2 * NCH + 10
 
 
 def kernel(
@@ -55,20 +57,20 @@
     for peer in peers:
         pl.semaphore_signal(barrier, inc=1, device_id=peer, device_id_type=MESH)
 
-    lane = lax.broadcasted_iota(jnp.int32, (ROWS, 128), 1)
-    expert_of = lane % 32
-    is_b = (lane // 32) % 2 == 1
-    chosen = jnp.zeros((ROWS, 128), F32)
-    weight = jnp.zeros((ROWS, 128), F32)
+    line = lax.broadcasted_iota(jnp.int32, (128, ROWS), 0)
+    expert_of = line % 32
+    is_b = (line // 32) % 2 == 1
+    chosen = jnp.zeros((128, ROWS), F32)
+    weight = jnp.zeros((128, ROWS), F32)
     for k in range(TOP):
-        named = jnp.where(is_b, routes_b[:, k : k + 1], routes_f[:, k : k + 1])
+        named = jnp.where(is_b, routes_b[k : k + 1, :], routes_f[k : k + 1, :])
         hit = named == expert_of
         chosen = jnp.where(hit, 1.0, chosen)
-        weight = jnp.where(hit, jnp.where(is_b, mix_b[:, k : k + 1], mix_f[:, k : k + 1]), weight)
-    earlier = lax.broadcasted_iota(jnp.int32, (ROWS, ROWS), 0) > lax.broadcasted_iota(jnp.int32, (ROWS, ROWS), 1)
-    rank = jnp.dot(jnp.where(earlier, 1.0, 0.0).astype(BF), chosen.astype(BF), preferred_element_type=F32)
+        weight = jnp.where(hit, jnp.where(is_b, mix_b[k : k + 1, :], mix_f[k : k + 1, :]), weight)
+    earlier = lax.broadcasted_iota(jnp.int32, (ROWS, ROWS), 0) < lax.broadcasted_iota(jnp.int32, (ROWS, ROWS), 1)
+    rank = jnp.dot(chosen.astype(BF), jnp.where(earlier, 1.0, 0.0).astype(BF), preferred_element_type=F32)
     slot = jnp.where(chosen > 0.5, rank + (z * CAP + 1).astype(F32), 0.0)
-    tab[0, x, z] = jnp.where(lane < 64, slot, weight)
+    tab[0, x, z] = jnp.where(line < 64, slot, weight).T
 
     def spread(array, wide):
         for v in range(2):
@@ -95,16 +97,15 @@
         for v in range(2):
             part = ag.at[n, v, :, z]
             send(part, part, b_s.at[n], b_r.at[n], other)
-        wait(six, a_s.at[n])
 
     def stage_c(n, array):
         batch = 1 if array < 2 else 0
-        ring = n % RING
+        ring = n % RING_S
         wait(ag.at[n, 0], b_r.at[n])
 
-        @pl.when(n >= RING)
+        @pl.when(n >= RING_S)
         def _():
-            wait(snd.at[ring], c_s.at[n - RING])
+            wait(snd.at[ring], c_s.at[n - RING_S])
 
         def one(q, carry):
             for v in range(2):
@@ -125,10 +126,9 @@
         for k in shifts:
             send(snd.at[ring, 0, k - 1], rc.at[n, 0, :, y], c_s.at[n], c_r.at[n], trade_peer(0, k))
             send(snd.at[ring, 1, k - 1], rc.at[n, 1, x], c_s.at[n], c_r.at[n], trade_peer(1, k))
-        wait(ag.at[n, 0], b_s.at[n])
-
-    def fetch(step, down):
-        j, ring = (step - 3) % NCH, step % 2
+
+    def fetch(i, down):
+        j, ring = i % NCH, i % 2
         for v in range(2):
             cols = pl.ds(pl.multiple_of(v * HALF + j * CH, CH), CH)
             if down:
@@ -136,23 +136,10 @@
             else:
                 pltpu.make_async_copy(wup.at[cols, :], wbu.at[ring, v], w_sem.at[ring]).start()
 
-    def fetched(step, down):
-        ring = step % 2
-        wait((wbd if down else wbu).at[ring], w_sem.at[ring])
-        return ring
-
-    def next_weights(step, last, down):
-        @pl.when(step < last)
-        def _():
-            fetch(step + 1, down)
-
-        @pl.when(step == last)
-        def _():
-            fetch(step + 1, not down)
-
     NT = (((1,), (1,)), ((), ()))
 
-    def stage_d(n, ring, down, total):
+    def stage_d(n, down, total):
+        ring = n % 2
         six = rc.at[n, :, pl.ds(0, 3)]
         wait(six, c_r.at[n])
 
@@ -169,12 +156,12 @@
 
         lax.fori_loop(0, SIDE, one, 0)
 
-    def stage_e(r, wring, down):
-        ring = r % RING
-
-        @pl.when(r >= RING)
+    def stage_e(r, down):
+        ring, wring = r % RING_O, r % 2
+
+        @pl.when(r >= RING_O)
         def _():
-            wait(ob.at[ring, :, pl.ds(0, 3)], e_s.at[r - RING])
+            wait(ob.at[ring, :, pl.ds(0, 3)], e_s.at[r - RING_O])
 
         def one(q, carry):
             for v in range(2):
@@ -194,13 +181,13 @@
         rc[r, 1, 0] = ob[ring, 1, x]
 
     def stage_f(r):
-        ring = r % RING
+        ring = r % RING_Z
         unit = r // NCH
         wait(rc.at[r, :, pl.ds(1, 3)], e_r.at[r])
 
-        @pl.when(r >= RING)
+        @pl.when(r >= RING_Z)
         def _():
-            wait(zb.at[ring, :, 0], f_s.at[r - RING])
+            wait(zb.at[ring, :, 0], f_s.at[r - RING_Z])
 
         def one(q, carry):
             for v in range(2):
@@ -216,20 +203,20 @@
             send(zb.at[ring, v, 1 - z], zr.at[r, v], f_s.at[r], f_r.at[r], other)
 
     def stage_g(r):
-        ring = r % RING
+        ring, zring = r % RING_X, r % RING_Z
         wait(zr.at[r], f_r.at[r])
 
-        @pl.when(r >= RING)
+        @pl.when(r >= RING_X)
         def _():
-            wait(xb.at[ring, :, pl.ds(0, 3)], g_s.at[r - RING])
-
-        for v in range(2):
-            xb[ring, v] = (zb[ring, v, z].astype(F32) + zr[r, v].astype(F32)).astype(BF)
+            wait(xb.at[ring, :, pl.ds(0, 3)], g_s.at[r - RING_X])
+
+        for v in range(2):
+            xb[ring, v] = (zb[zring, v, z].astype(F32) + zr[r, v].astype(F32)).astype(BF)
             for k in shifts:
                 send(xb.at[ring, v, (gather_at[v] + k) % SIDE], xr.at[r, v, k - 1], g_s.at[r], g_r.at[r], gather_peer(v, k))
 
     def summed(r, v):
-        out = xb[r % RING, v, gather_at[v]].astype(F32)
+        out = xb[r % RING_X, v, gather_at[v]].astype(F32)
         for k in range(SIDE - 1):
             out = out + xr[r, v, k].astype(F32)
         return out
@@ -265,34 +252,33 @@
                 gb[:, lo : lo + CH] = (cot[:, lo : lo + CH].astype(F32) + g_x).astype(BF)
         send(gb, next_b, p_s.at[1], p_r.at[1], behind)
 
+    def when(condition, stage, *args):
+        pl.when(condition)(lambda: stage(*args))
+
+    def within(i, lo, hi):
+        return jnp.logical_and(i >= lo, i < hi)
+
     pl.semaphore_wait(barrier, len(peers))
     send(tab.at[0, x, z], tab.at[0, x, z], t_s.at[0], t_r.at[0], other)
     stage_a(0)
-    fetch(3, False)
+    fetch(0, False)
     spread(1, cot[...])
-    stage_a(1)
     wait(tab.at[0, 0, 0], t_r.at[0])
     wait(tab.at[0, 0, 0], t_s.at[0])
     tab[1, y] = tab[0, x]
     for v in range(2):
         for k in shifts:
             send(tab.at[v, gather_at[v]], tab.at[v, gather_at[v]], t_s.at[1], t_r.at[1], gather_peer(v, k))
-    stage_b(0)
     spread(2, normed(act)[0] * gain[...])
-    stage_b(1)
-    stage_a(2)
     acc[...] = jnp.zeros_like(acc)
     gh[...] = jnp.zeros_like(gh)
-    six = tab.at[:, pl.ds(0, 3)]
-    wait(six, t_r.at[1])
-    wait(six, t_s.at[1])
 
     slot_row = lax.broadcasted_iota(jnp.int32, (PAIR, 128), 0).astype(F32) + 1.0
     token_lane = lax.broadcasted_iota(jnp.int32, (PT, 128), 1)
     w_lane = lax.broadcasted_iota(jnp.int32, (PT, LINE), 1)
     w_slot = (w_lane % PAIR).astype(F32) + 1.0
 
-    def tables(q, carry):
+    def one_table(q, carry):
         for v in range(2):
             pair = tab[v, q].reshape(PT, 128)
             ttab[v] = pair.T
@@ -322,142 +308,79 @@
             cw[0, v, q, PT:] = jnp.zeros((PT, LINE), BF)
         return carry
 
-    lax.fori_loop(0, SIDE, tables, 0)
-    stage_c(0, 0)
-
-    s1 = 3 + NCH
-    s2 = s1 + NCH
-    s3 = s2 + NCH
-    s4 = s3 + NCH
-
-    def loop1(s, carry):
-        stage_b(s - 1)
-        stage_a(s)
-
-        @pl.when(s - 2 < NCH)
-        def _():
-            stage_c(s - 2, 0)
-
-        @pl.when(s - 2 >= NCH)
-        def _():
-            stage_c(s - 2, 1)
-
-        next_weights(s, s1 - 1, False)
-        stage_d(s - 3, fetched(s, False), False, acc)
+    def tables():
+        six = tab.at[:, pl.ds(0, 3)]
+        wait(six, t_r.at[1])
+        wait(six, t_s.at[1])
+        lax.fori_loop(0, SIDE, one_table, 0)
+
+    def between_b():
+        def one(q, carry):
+            p = acc[q]
+            sigma = jax.nn.sigmoid(p)
+            hid[q] = (gh[q] * sigma * (1.0 + p * (1.0 - sigma))).astype(BF)
+            acc[q] = jnp.zeros_like(p)
+            return carry
+
+        lax.fori_loop(0, SIDE, one, 0)
+
+    def between_f():
+        def one(q, carry):
+            p = acc[q]
+            hid[q] = (p * jax.nn.sigmoid(p)).astype(BF)
+            return carry
+
+        lax.fori_loop(0, SIDE, one, 0)
+
+    def step(s, carry):
+        when(within(s - AT_B, 0, NOUT), stage_b, s - AT_B)
+        when(within(s - AT_F, 0, NRET), stage_f, s - AT_F)
+        when(within(s - AT_A, 1, NOUT), stage_a, s - AT_A)
+        when(within(s - AT_G, 0, NRET), stage_g, s - AT_G)
+
+        when(s == AT_C, tables)
+        n = s - AT_C
+        when(within(n, 0, NCH), stage_c, n, 0)
+        when(within(n, NCH, 2 * NCH), stage_c, n, 1)
+        when(within(n, 2 * NCH, NOUT), stage_c, n, 2)
+
+        i = s - AT_D
+        for down in (False, True):
+            kind = (i // NCH) % 2 == (1 if down else 0)
+            kind_next = ((i + 1) // NCH) % 2 == (1 if down else 0)
+            when(jnp.logical_and(within(i, 0, 4 * NCH - 1), kind_next), fetch, i + 1, down)
+            now = jnp.logical_and(within(i, 0, 4 * NCH), kind)
+            when(now, lambda down=down: wait((wbd if down else wbu).at[i % 2], w_sem.at[i % 2]))
+        when(i == 2 * NCH, between_b)
+        when(i == 3 * NCH, between_f)
+        when(within(i, 2 * NCH, 3 * NCH), stage_e, i - 2 * NCH, False)
+        when(within(i, 3 * NCH, 4 * NCH), stage_e, i - 2 * NCH, True)
+        when(within(i, 0, NCH), stage_d, i, False, acc)
+        when(within(i, NCH, 2 * NCH), stage_d, i, True, gh)
+        when(within(i, 2 * NCH, NOUT), stage_d, i, False, acc)
+
+        r = s - AT_H
+        when(within(r, 0, NCH), stage_h_b, r)
+        when(within(r, NCH, NRET), stage_h_f, r)
+        when(r == NCH, finish_b)
         return carry
 
-    lax.fori_loop(3, s1, loop1, 0)
-
-    def loop2(s, carry):
-        stage_b(s - 1)
-        stage_a(s)
-
-        @pl.when(s - 2 < 2 * NCH)
-        def _():
-            stage_c(s - 2, 1)
-
-        @pl.when(s - 2 >= 2 * NCH)
-        def _():
-            stage_c(s - 2, 2)
-
-        next_weights(s, s2 - 1, True)
-        stage_d(s - 3, fetched(s, True), True, gh)
+    lax.fori_loop(0, AT_H + NRET, step, 0)
+
+    def sent(n, carry):
+        wait(ag.at[0, 0, pl.ds(0, 3)], a_s.at[n])
+        wait(ag.at[0, 0], b_s.at[n])
         return carry
 
-    lax.fori_loop(s1, s2, loop2, 0)
-
-    def between_b(q, carry):
-        p = acc[q]
-        sigma = jax.nn.sigmoid(p)
-        hid[q] = (gh[q] * sigma * (1.0 + p * (1.0 - sigma))).astype(BF)
-        acc[q] = jnp.zeros_like(p)
-        return carry
-
-    lax.fori_loop(0, SIDE, between_b, 0)
-
-    def back(s):
-        r = s - s2
-
-        @pl.when(r >= 1)
-        def _():
-            stage_f(r - 1)
-
-        @pl.when(r >= 2)
-        def _():
-            stage_g(r - 2)
-
-    def loop3(s, carry):
-        @pl.when(s - 1 < NOUT)
-        def _():
-            stage_b(s - 1)
-
-        @pl.when(s < NOUT)
-        def _():
-            stage_a(s)
-
-        @pl.when(s - 2 < NOUT)
-        def _():
-            stage_c(s - 2, 2)
-
-        next_weights(s, s3 - 1, False)
-        ring = fetched(s, False)
-        stage_e(s - s2, ring, False)
-        stage_d(s - 3, ring, False, acc)
-        back(s)
-
-        @pl.when(s - s2 >= 3)
-        def _():
-            stage_h_b(s - s2 - 3)
-
-        return carry
-
-    lax.fori_loop(s2, s3, loop3, 0)
-
-    def between_f(q, carry):
-        p = acc[q]
-        hid[q] = (p * jax.nn.sigmoid(p)).astype(BF)
-        return carry
-
-    lax.fori_loop(0, SIDE, between_f, 0)
-
-    def loop4(s, carry):
-        @pl.when(s < s4 - 1)
-        def _():
-            fetch(s + 1, True)
-
-        ring = fetched(s, True)
-        stage_e(s - s2, ring, True)
-        back(s)
-        r = s - s2 - 3
-
-        @pl.when(r < NCH)
-        def _():
-            stage_h_b(r)
-
-        @pl.when(r >= NCH)
-        def _():
-            stage_h_f(r)
-
-        @pl.when(r == NCH)
-        def _():
-            finish_b()
-
-        return carry
-
-    lax.fori_loop(s3, s4, loop4, 0)
-    stage_f(NRET - 1)
-    stage_g(NRET - 2)
-    stage_h_f(NRET - 3)
-    stage_g(NRET - 1)
-    stage_h_f(NRET - 2)
-    stage_h_f(NRET - 1)
-
-    for n in range(NOUT - RING, NOUT):
-        wait(snd.at[n % RING], c_s.at[n])
-    for r in range(NRET - RING, NRET):
-        wait(ob.at[r % RING, :, pl.ds(0, 3)], e_s.at[r])
-        wait(zb.at[r % RING, :, 0], f_s.at[r])
-        wait(xb.at[r % RING, :, pl.ds(0, 3)], g_s.at[r])
+    lax.fori_loop(0, NOUT, sent, 0)
+    for n in range(NOUT - RING_S, NOUT):
+        wait(snd.at[0], c_s.at[n])
+    for r in range(NRET - RING_O, NRET):
+        wait(ob.at[0, :, pl.ds(0, 3)], e_s.at[r])
+    for r in range(NRET - RING_Z, NRET):
+        wait(zb.at[0, :, 0], f_s.at[r])
+    for r in range(NRET - RING_X, NRET):
+        wait(xb.at[0, :, pl.ds(0, 3)], g_s.at[r])
     wait(gb, p_s.at[0])
     wait(gb, p_s.at[1])
     wait(next_f, p_r.at[0])
@@ -479,13 +402,13 @@
         scratch_shapes=[
             pltpu.VMEM((NOUT, 2, SIDE, DEEP, ROWS, CH), BF),
             pltpu.VMEM((NOUT, 2, SIDE, SIDE, PAIR, CH), BF),
-            pltpu.VMEM((RING, 2, SIDE - 1, SIDE, PAIR, CH), BF),
+            pltpu.VMEM((RING_S, 2, SIDE - 1, SIDE, PAIR, CH), BF),
             pltpu.VMEM((2, 2, CH, HID), BF),
             pltpu.VMEM((2, 2, HID, CH), BF),
-            pltpu.VMEM((RING, 2, SIDE, SIDE, PAIR, CH), BF),
-            pltpu.VMEM((RING, 2, DEEP, SIDE, ROWS, CH), BF),
+            pltpu.VMEM((RING_O, 2, SIDE, SIDE, PAIR, CH), BF),
+            pltpu.VMEM((RING_Z, 2, DEEP, SIDE, ROWS, CH), BF),
             pltpu.VMEM((NRET, 2, SIDE, ROWS, CH), BF),
-            pltpu.VMEM((RING, 2, SIDE, ROWS, CH), BF),
+            pltpu.VMEM((RING_X, 2, SIDE, ROWS, CH), BF),
             pltpu.VMEM((NRET, 2, SIDE - 1, ROWS, CH), BF),
             pltpu.VMEM((NCH, 2, ROWS, CH), F32),
             pltpu.VMEM((SIDE, LINE, HID), F32),
@@ -505,7 +428,7 @@
         ),
         cost_estimate=pl.CostEstimate(flops=30 * 10**9, bytes_accessed=40 * 10**6, transcendentals=2 * 10**6),
     )(
-        act_fwd[0], routes_fwd[0], mix_fwd[0], cot_bwd[0], saved_bwd[0], routes_bwd[0], mix_bwd[0],
+        act_fwd[0], routes_fwd[0].T, mix_fwd[0].T, cot_bwd[0], saved_bwd[0], routes_bwd[0].T, mix_bwd[0].T,
         norm_gain, w_up[0, 0], w_down[0, 0],
     )
     return next_fwd[None], next_bwd[None]

time: 256 us -> 231 us (0.902)
  Pallas kernels: 243 us -> 224 us
  local copies, waits for them, and re-layouts: 9.16 us -> 3.63 us
    pallas_call x1, Pallas kernels: 243 us -> 224 us  [per_device(): pl.pallas_call(kernel, out_shape=(out, out), in_specs=[vmem] * 8 + [far]...]
    unnamed x6 -> x2, local copies, waits for them, and re-layouts: 9.16 us -> 3.63 us
where the time goes in v2:
time: 231 us; the launch traced here: 229 us
  Pallas kernels  224 us (97%)
  local copies, waits for them, and re-layouts  3.63 us (2%)
    pallas_call x1, Pallas kernels, per_device(): pl.pallas_call(kernel, out_shape=(out, out), in_specs=[vmem] * 8 + [far]...  224 us

profile of v2, /device:TPU:6, one launch (start us, length us, event | category | flops | bytes accessed | tf_op | source)
XLA Modules:
  0.0 228.6 jit_solution(14596579359176346114)
XLA Ops:
  0.6 224.3 %shard_map.113 = (bf16[64,3584]{1,0:T(8,128)(2,1)}, bf16[64,3584]{1,0:T(8,128)(2,1)}) custom-call(bf16[64,3584]{1,0:T(8,128)(2,1)} %bitcast.23, s32[8,64]{1,0:T(8,128)} %bitcast.26, f32[8,64]{1,0:T(8,128)} %bitcast.27, bf16[64,3584]{1,0:T(8,128)(2,1)} %bitcast.24, bf16[64,3584]{1,0:T(8,128)(2,1)} %bitcast.25, s32[8,64]{1,0:T(8,128)} %bitcast.28, ...), custom_call_target="tpu_custom_call" | custom-call | flops 30000001024 | bytes 40000000 | tf_op jit(solution)/shard_map/pallas_call | solution.py:397
  224.9 1.8 copy.14
  226.7 1.8 copy.15

commit v3 on v2

v3 whole, which is shorter than its diff:
```python
import functools

import jax
import jax.numpy as jnp
from jax import lax
from jax.experimental import pallas as pl
from jax.experimental.pallas import tpu as pltpu
from jax.sharding import PartitionSpec as P

MESH = pl.DeviceIdType.MESH
BF, F32 = jnp.bfloat16, jnp.float32

D, HID, TOP, ROWS, CAP = 3584, 1024, 8, 64, 24
SIDE, DEEP = 4, 2
HALF = D // 2
CH = 256
NCH = HALF // CH
PAIR = DEEP * CAP
LINE = SIDE * PAIR
PT = DEEP * ROWS
NOUT, NRET = 3 * NCH, 2 * NCH
RING_S, RING_O, RING_Z, RING_X = 3, 4, 7, 5
LAST = NRET - 1
AT_A, AT_B, AT_W, AT_C, AT_D = 0, 2, 3, 6, 7
AT_E = AT_D + 2 * NCH
AT_F, AT_G, AT_V, AT_H = AT_E + 2, AT_E + 5, AT_E + 7, AT_E + 11
SLOT = {0: 1, 1: 2, 2: 3, 3: 0}


def late(n):
    return n < 0


def kernel(
    act_far, routes_f, mix_f, cot_far, saved_far, routes_b, mix_b, gain, wup, wdn,
    both_next,
    act, cot, saved, i_s, xl,
    ag, rc, snd, wbu, wbd, ob, zb, zr, xb, xr, gs, acc, gh, hid, sel, scl, cw, tab, own_tab, far_tab, pair_tab, xf,
    a_s, a_r, b_s, b_r, c_s, c_r, e_s, e_r, f_s, f_r, g_s, g_r, h_s, h_r, k_s, k_r, v_s, v_r, w_sem, t_s, t_r, p_s, p_r,
):
    next_f, next_b = both_next.at[0], both_next.at[1]
    pp, me = lax.axis_index("pipe"), lax.axis_index("expert")
    z, x, y = me // (SIDE * SIDE), (me // SIDE) % SIDE, me % SIDE
    n_pipe = lax.axis_size("pipe")

    def device(dz, dx, dy):
        return (pp, ((z + dz) % DEEP) * SIDE * SIDE + ((x + dx) % SIDE) * SIDE + (y + dy) % SIDE)

    gather_at, trade_at = (x, y), (y, x)
    gather_peer = lambda v, k: device(0, k, 0) if v == 0 else device(0, 0, k)
    trade_peer = lambda v, k: device(0, 0, k) if v == 0 else device(0, k, 0)
    other = device(1, 0, 0)
    ahead, behind = ((pp + 1) % n_pipe, me), ((pp + n_pipe - 1) % n_pipe, me)
    shifts = range(1, SIDE)

    def send(src, dst, s_sem, r_sem, to):
        pltpu.make_async_remote_copy(
            src_ref=src, dst_ref=dst, send_sem=s_sem, recv_sem=r_sem, device_id=to, device_id_type=MESH
        ).start()

    def wait(ref, sem):
        pltpu.make_async_copy(ref, ref, sem).wait()

    barrier = pltpu.get_barrier_semaphore()
    peers = [other, ahead, behind] + [gather_peer(v, k) for v in range(2) for k in shifts]
    for peer in peers:
        pl.semaphore_signal(barrier, inc=1, device_id=peer, device_id_type=MESH)

    loads = [pltpu.make_async_copy(far, near, i_s.at[i]) for i, (far, near) in enumerate(((saved_far, saved), (cot_far, cot), (act_far, act)))]
    for load in loads:
        load.start()

    line = lax.broadcasted_iota(jnp.int32, (128, PT), 0)
    mine = lax.broadcasted_iota(jnp.int32, (128, PT), 1) // ROWS == z
    major, minor, field = (line // 16) % SIDE, (line // 4) % SIDE, line % 4
    is_b = field % 2 == 1
    earlier = lax.broadcasted_iota(jnp.int32, (PT, PT), 0) < lax.broadcasted_iota(jnp.int32, (PT, PT), 1)
    earlier = jnp.where(earlier, 1.0, 0.0).astype(BF)
    twice = lambda ref, k: jnp.concatenate([ref[k : k + 1, :]] * DEEP, axis=1)
    for v in range(2):
        expert_of = (line // 64) * SIDE * SIDE + (major * SIDE + minor if v == 0 else minor * SIDE + major)
        chosen = jnp.zeros((128, PT), F32)
        weight = jnp.zeros((128, PT), F32)
        for k in range(TOP):
            hit = jnp.logical_and(jnp.where(is_b, twice(routes_b, k), twice(routes_f, k)) == expert_of, mine)
            chosen = jnp.where(hit, 1.0, chosen)
            weight = jnp.where(hit, jnp.where(is_b, twice(mix_b, k), twice(mix_f, k)), weight)
        rank = jnp.dot(chosen.astype(BF), earlier, preferred_element_type=F32)
        slot = jnp.where(chosen > 0.5, rank + (z * CAP + 1).astype(F32), 0.0)
        table = jnp.where(field < 2, slot, weight)
        for zz in range(DEEP):
            own_tab[v, zz] = table[zz * 64 : (zz + 1) * 64].reshape(SIDE, 16, PT)

    def spread(array, wide):
        for v in range(2):
            for j in range(NCH):
                lo = v * HALF + j * CH
                ag[array * NCH + j, v, 1, z] = wide[:, lo : lo + CH].astype(BF)

    def normed(ref):
        wide = ref[...].astype(F32)
        recip = lax.rsqrt(jnp.sum(wide * wide, axis=-1, keepdims=True) * (1.0 / D) + 1e-06)
        return wide * recip, recip

    loads[0].wait()
    spread(0, normed(saved)[0] * gain[...])

    def choose(n, early, after):
        pl.when(late(n))(after)
        pl.when(jnp.logical_not(late(n)))(early)

    top, bottom = pl.ds(0, ROWS // 2), pl.ds(ROWS // 2, ROWS // 2)

    def stage_a(n):
        for v in range(2):
            own = ag.at[n, v, 1, z]
            send(own, ag.at[n, v, 0, z], a_s.at[n], a_r.at[n], gather_peer(v, 1))
            send(own, ag.at[n, v, 2, z], a_s.at[n], a_r.at[n], gather_peer(v, 3))

    def stage_b(n):
        wait(ag.at[n, 0, pl.ds(0, 2)], a_r.at[n])
        for v in range(2):
            part = ag.at[n, v, pl.ds(0, 3), z]
            send(part, part, b_s.at[n], b_r.at[n], other)

        @pl.when(jnp.logical_not(late(n)))
        def _():
            for v in range(2):
                send(ag.at[n, v, 0, z, top], ag.at[n, v, 3, z, top], h_s.at[n], h_r.at[n], gather_peer(v, 1))
                send(ag.at[n, v, 2, z, bottom], ag.at[n, v, 3, z, bottom], h_s.at[n], h_r.at[n], gather_peer(v, 3))

    def stage_w(n):
        def early():
            wait(ag.at[n, :, 3, 0], h_r.at[n])
            for v in range(2):
                send(ag.at[n, v, 3, z], ag.at[n, v, 3, z], k_s.at[n], k_r.at[n], other)

        def after():
            wait(ag.at[n, :, pl.ds(0, 3), 0], b_r.at[n])
            for v in range(2):
                send(ag.at[n, v, 0, :, top], ag.at[n, v, 3, :, top], h_s.at[n], h_r.at[n], gather_peer(v, 1))
                send(ag.at[n, v, 2, :, bottom], ag.at[n, v, 3, :, bottom], h_s.at[n], h_r.at[n], gather_peer(v, 3))

        choose(n, early, after)

    def gathered(n):
        def early():
            wait(ag.at[n, :, pl.ds(0, 3), 0], b_r.at[n])
            wait(ag.at[n, :, 3, 0], k_r.at[n])

        choose(n, early, lambda: wait(ag.at[n, :, 3], h_r.at[n]))

    def first_a():
        for v in range(2):
            own = ag.at[0, v, 1, z]
            send(own, own, a_s.at[0], a_r.at[0], other)

    def first_b():
        wait(ag.at[0, 0, 0], a_r.at[0])
        for v in range(2):
            for k in shifts:
                send(ag.at[0, v, 1], ag.at[0, v, SLOT[SIDE - k]], b_s.at[0], b_r.at[0], gather_peer(v, k))

    def stage_c(n, array):
        batch = 1 if array < 2 else 0
        ring = n % RING_S
        if array == 0:
            pl.when(n == 0)(lambda: wait(ag.at[0, :, pl.ds(0, 3)], b_r.at[0]))
            pl.when(n > 0)(lambda: gathered(n))
        else:
            gathered(n)

        @pl.when(n >= RING_S)
        def _():
            wait(snd.at[ring], c_s.at[n - RING_S])

        def one(i, carry):
            for v in range(2):
                q = (gather_at[v] + i + SIDE - 1) % SIDE
                rows = ag[n, v, i].reshape(PT, CH)
                got = jnp.dot(sel[batch, v, i], rows, preferred_element_type=F32)
                if array == 1:
                    got = got * scl[v, i][:, 0:1]
                got = got.astype(BF).reshape(SIDE, PAIR, CH)
                if v == 0:
                    rc[n, 0, q, y] = got[0]
                else:
                    rc[n, 1, x, q] = got[0]
                for d in shifts:
                    snd[ring, v, d - 1, q] = got[d]
            return carry

        lax.fori_loop(0, SIDE, one, 0)
        for k in shifts:
            send(snd.at[ring, 0, k - 1], rc.at[n, 0, :, y], c_s.at[n], c_r.at[n], trade_peer(0, k))
            send(snd.at[ring, 1, k - 1], rc.at[n, 1, x], c_s.at[n], c_r.at[n], trade_peer(1, k))

    def fetch(i, down):
        j, ring = i % NCH, i % 2
        for v in range(2):
            cols = pl.ds(pl.multiple_of(v * HALF + j * CH, CH), CH)
            if down:
                pltpu.make_async_copy(wdn.at[:, cols], wbd.at[ring, v], w_sem.at[ring]).start()
            else:
                pltpu.make_async_copy(wup.at[cols, :], wbu.at[ring, v], w_sem.at[ring]).start()

    NT = (((1,), (1,)), ((), ()))

    def stage_d(n, down, total):
        ring = n % 2
        six = rc.at[n, :, pl.ds(0, 3)]
        wait(six, c_r.at[n])

        def one(q, carry):
            out = total[q]
            for v in range(2):
                rows = rc[n, v, q].reshape(LINE, CH)
                if down:
                    out = out + lax.dot_general(rows, wbd[ring, v], NT, preferred_element_type=F32)
                else:
                    out = out + jnp.dot(rows, wbu[ring, v], preferred_element_type=F32)
            total[q] = out
            return carry

        lax.fori_loop(0, SIDE, one, 0)

    def stage_e(r, down):
        ring, wring = r % RING_O, r % 2

        @pl.when(r >= RING_O)
        def _():
            wait(ob.at[ring, :, pl.ds(0, 3)], e_s.at[r - RING_O])

        def one(q, carry):
            for v in range(2):
                if down:
                    got = jnp.dot(hid[q], wbd[wring, v], preferred_element_type=F32)
                else:
                    got = lax.dot_general(hid[q], wbu[wring, v], NT, preferred_element_type=F32)
                ob[ring, v, q] = got.astype(BF).reshape(SIDE, PAIR, CH)
            return carry

        lax.fori_loop(0, SIDE, one, 0)
        for k in shifts:
            send(ob.at[ring, 0, :, (y + k) % SIDE], rc.at[r, 0, SIDE - k], e_s.at[r], e_r.at[r], trade_peer(0, k))
            send(ob.at[ring, 1, (x + k) % SIDE], rc.at[r, 1, SIDE - k], e_s.at[r], e_r.at[r], trade_peer(1, k))
        for q in range(SIDE):
            rc[r, 0, 0, q] = ob[ring, 0, q, y]
        rc[r, 1, 0] = ob[ring, 1, x]

    def combine(r):
        ring = r % RING_Z
        unit = r // NCH
        wait(rc.at[r, :, pl.ds(1, 3)], e_r.at[r])

        @pl.when(r >= RING_Z)
        def _():
            sent_back(r - RING_Z)

        def one(i, carry):
            for v in range(2):
                q = (gather_at[v] + i + SIDE - 1) % SIDE
                rows = rc[r, v, :, q].reshape(LINE, CH)
                both = jnp.dot(cw[unit, v, i], rows, preferred_element_type=F32)
                part = (both[:PT] + both[PT:]).astype(BF).reshape(DEEP, ROWS, CH)
                for zz in range(DEEP):
                    zb[ring, v, zz, i] = part[zz]
            return carry

        lax.fori_loop(0, SIDE, one, 0)

    def sent_back(r):
        def early():
            wait(zb.at[0, :, 0], f_s.at[r])

        def after():
            wait(zb.at[0, :, :, 3], v_s.at[r])
            wait(zb.at[0, :, 0, pl.ds(0, 3)], f_s.at[r])

        choose(r, early, after)

    def stage_f(r):
        combine(r)
        ring = r % RING_Z

        def early():
            for v in range(2):
                send(zb.at[ring, v, 1 - z], zr.at[r, v], f_s.at[r], f_r.at[r], other)

        def after():
            for v in range(2):
                send(zb.at[ring, v, :, 3, top], xf.at[r, v, 0], v_s.at[r], v_r.at[r], gather_peer(v, 1))
                send(zb.at[ring, v, :, 3, bottom], xf.at[r, v, 1], v_s.at[r], v_r.at[r], gather_peer(v, 3))

        choose(r, early, after)

    def stage_g(r):
        ring, xring = r % RING_Z, r % RING_X

        @pl.when(r >= RING_X)
        def _():
            wait(xb.at[0, :, pl.ds(0, 2)], g_s.at[r - RING_X])
            pl.when(jnp.logical_not(late(r - RING_X)))(lambda: wait(xb.at[0, :, 0], v_s.at[r - RING_X]))

        def early():
            wait(zr.at[r], f_r.at[r])
            for v in range(2):
                xb[xring, v, 3] = (zb[ring, v, z, 3].astype(F32) + zr[r, v, 3].astype(F32)).astype(BF)
                send(xb.at[xring, v, 3, top], xf.at[r, v, 0, 0], v_s.at[r], v_r.at[r], gather_peer(v, 1))
                send(xb.at[xring, v, 3, bottom], xf.at[r, v, 1, 0], v_s.at[r], v_r.at[r], gather_peer(v, 3))

        def after():
            wait(xf.at[r], v_r.at[r])
            for v in range(2):
                for zz in range(DEEP):
                    zb[ring, v, zz, 2, top] = (zb[ring, v, zz, 2, top].astype(F32) + xf[r, v, 0, zz].astype(F32)).astype(BF)
                    zb[ring, v, zz, 0, bottom] = (zb[ring, v, zz, 0, bottom].astype(F32) + xf[r, v, 1, zz].astype(F32)).astype(BF)
                part = pl.ds(0, 3)
                send(zb.at[ring, v, 1 - z, part], zr.at[r, v, part], f_s.at[r], f_r.at[r], other)

        choose(r, early, after)

    def stage_v(r):
        ring, xring = r % RING_Z, r % RING_X
        choose(r, lambda: wait(xf.at[r, :, :, 0], v_r.at[r]), lambda: wait(zr.at[r, :, pl.ds(0, 3)], f_r.at[r]))
        for v in range(2):
            for i in range(3):
                xb[xring, v, i] = (zb[ring, v, z, i].astype(F32) + zr[r, v, i].astype(F32)).astype(BF)

            @pl.when(jnp.logical_not(late(r)))
            def _():
                for i, rows, j in ((2, top, 0), (0, bottom, 1)):
                    xb[xring, v, i, rows] = (
                        zb[ring, v, z, i, rows].astype(F32) + zr[r, v, i, rows].astype(F32) + xf[r, v, j, 0].astype(F32)
                    ).astype(BF)

            send(xb.at[xring, v, 2], xr.at[r, v, 0], g_s.at[r], g_r.at[r], gather_peer(v, 1))
            send(xb.at[xring, v, 0], xr.at[r, v, 1], g_s.at[r], g_r.at[r], gather_peer(v, 3))

    xz = wbu.at[0]
    half = lambda zz: pl.ds(pl.multiple_of(zz * ROWS, ROWS), ROWS)

    def last_f():
        combine(LAST)
        for v in range(2):
            for k in shifts:
                part = zb.at[LAST % RING_Z, v, :, SLOT[k]]
                send(part, xl.at[v, k - 1], f_s.at[LAST], f_r.at[LAST], gather_peer(v, k))

    def last_g():
        wait(xl, f_r.at[LAST])
        for v in range(2):
            for zz in range(DEEP):
                out = zb[LAST % RING_Z, v, zz, 1].astype(F32)
                for k in range(SIDE - 1):
                    out = out + xl[v, k, zz].astype(F32)
                xz[v, zz * ROWS : (zz + 1) * ROWS, :CH] = out.astype(BF)
            send(xz.at[v, half(1 - z), pl.ds(0, CH)], xr.at[LAST, v, 0], g_s.at[LAST], g_r.at[LAST], other)

    def summed(r, v):
        return xb[r % RING_X, v, 1].astype(F32) + xr[r, v, 0].astype(F32) + xr[r, v, 1].astype(F32)

    def stage_h_b(r):
        wait(xr.at[r], g_r.at[r])
        for v in range(2):
            gs[r, v] = summed(r, v)

    def last_sum(r, v):
        return xz[v, half(z), :CH].astype(F32) + xr[LAST, v, 0].astype(F32)

    def stage_h_f(r, total=summed):
        if total is summed:
            wait(xr.at[r], g_r.at[r])
        else:
            wait(xr.at[LAST, :, 0], g_r.at[LAST])
        j = r - NCH
        for v in range(2):
            cols = pl.ds(pl.multiple_of(v * HALF + j * CH, CH), CH)
            act[:, cols] = (act[:, cols].astype(F32) + total(r, v)).astype(BF)
            send(act.at[:, cols], next_f.at[:, cols], p_s.at[0], p_r.at[0], ahead)

    def finish_b():
        scaled, recip = normed(saved)
        total = jnp.zeros((ROWS, 1), F32)
        parts = []
        for v in range(2):
            for j in range(NCH):
                lo = v * HALF + j * CH
                g_n = gs[j, v] * gain[:, lo : lo + CH]
                gs[j, v] = g_n
                total = total + jnp.sum(g_n * scaled[:, lo : lo + CH], axis=-1, keepdims=True)
        mean = total * (1.0 / D)
        for v in range(2):
            for j in range(NCH):
                lo = v * HALF + j * CH
                g_x = recip * (gs[j, v] - scaled[:, lo : lo + CH] * mean)
                cot[:, lo : lo + CH] = (cot[:, lo : lo + CH].astype(F32) + g_x).astype(BF)
        send(cot, next_b, p_s.at[1], p_r.at[1], behind)

    def when(condition, stage, *args):
        pl.when(condition)(lambda: stage(*args))

    def within(i, lo, hi):
        return jnp.logical_and(i >= lo, i < hi)

    pl.semaphore_wait(barrier, len(peers))
    first_a()
    send(own_tab.at[:, 1 - z], far_tab, t_s.at[0], t_r.at[0], other)
    stage_a(1)
    fetch(0, False)
    first_b()
    wait(far_tab, t_r.at[0])
    for v in range(2):
        pair_tab[v] = own_tab[v, z] + far_tab[v]
        tab[v, 1] = pair_tab[v, gather_at[v]]
        for k in shifts:
            part = pair_tab.at[v, (gather_at[v] + k) % SIDE]
            send(part, tab.at[v, SLOT[SIDE - k]], t_s.at[1], t_r.at[1], gather_peer(v, k))

    slot_row = lax.broadcasted_iota(jnp.int32, (PAIR, 128), 0).astype(F32) + 1.0
    def trade_row(v, d, field):
        return pl.ds(((trade_at[v] + d) % SIDE) * 4 + field, 1)

    def pick_tables(batch):
        def one(i, carry):
            for v in range(2):
                for d in range(SIDE):
                    hit = tab[v, i, trade_row(v, d, batch), :] == slot_row
                    sel[batch, v, i, d * PAIR : (d + 1) * PAIR, :] = jnp.where(hit, 1.0, 0.0).astype(BF)
            return carry

        lax.fori_loop(0, SIDE, one, 0)

    def scale_tables():
        def one(i, carry):
            for v in range(2):
                for d in range(SIDE):
                    gate = tab[v, i, trade_row(v, d, 3), :]
                    picked = sel[1, v, i, d * PAIR : (d + 1) * PAIR, :].astype(F32) * gate
                    scl[v, i, d * PAIR : (d + 1) * PAIR, :] = jnp.broadcast_to(
                        jnp.sum(picked, axis=1, keepdims=True), (PAIR, 128)
                    )
            return carry

        lax.fori_loop(0, SIDE, one, 0)

    def sum_tables(i):
        rest = jnp.zeros((2 * PT - LINE, PT), F32)
        for v in range(2):
            ones, gates = [], []
            for d in range(SIDE):
                ones.append(jnp.where(tab[v, i, trade_row(v, d, 1), :] == slot_row, 1.0, 0.0))
                hit = tab[v, i, trade_row(v, d, 0), :] == slot_row
                gates.append(jnp.where(hit, tab[v, i, trade_row(v, d, 2), :], 0.0))
            gate = jnp.concatenate(gates + [rest], axis=0).T[:, :LINE]
            one = jnp.concatenate(ones + [rest], axis=0).T[:, :LINE]
            high = gate.astype(BF)
            cw[1, v, i, :PT] = high
            cw[1, v, i, PT:] = (gate - high.astype(F32)).astype(BF)
            cw[0, v, i, :PT] = one.astype(BF)
            cw[0, v, i, PT:] = jnp.zeros((PT, LINE), BF)

    def tables():
        wait(tab.at[:, pl.ds(0, 3)], t_r.at[1])
        pick_tables(1)

    def load_cot():
        loads[1].wait()
        spread(1, cot[...])

    def load_act():
        loads[2].wait()
        spread(2, normed(act)[0] * gain[...])

    def clear():
        acc[...] = jnp.zeros_like(acc)
        gh[...] = jnp.zeros_like(gh)

    def between_b():
        def one(q, carry):
            p = acc[q]
            sigma = jax.nn.sigmoid(p)
            hid[q] = (gh[q] * sigma * (1.0 + p * (1.0 - sigma))).astype(BF)
            acc[q] = jnp.zeros_like(p)
            return carry

        lax.fori_loop(0, SIDE, one, 0)

    def between_f():
        def one(q, carry):
            p = acc[q]
            hid[q] = (p * jax.nn.sigmoid(p)).astype(BF)
            return carry

        lax.fori_loop(0, SIDE, one, 0)

    def step(s, carry):
        when(within(s - AT_B, 1, NOUT), stage_b, s - AT_B)
        when(within(s - AT_F, 0, LAST), stage_f, s - AT_F)
        when(s - AT_F == LAST, last_f)
        when(within(s - AT_W, 1, NOUT), stage_w, s - AT_W)
        when(within(s - AT_A, 2, NOUT), stage_a, s - AT_A)
        when(within(s - AT_V, 0, LAST), stage_v, s - AT_V)
        when(within(s - AT_G, 0, LAST), stage_g, s - AT_G)
        when(s - AT_G == LAST, last_g)

        when(s == AT_C, tables)
        n = s - AT_C
        when(within(n, 0, NCH), stage_c, n, 0)
        when(within(n, NCH, 2 * NCH), stage_c, n, 1)
        when(within(n, 2 * NCH, NOUT), stage_c, n, 2)

        i = s - AT_D
        for down in (False, True):
            kind = (i // NCH) % 2 == (1 if down else 0)
            kind_next = ((i + 1) // NCH) % 2 == (1 if down else 0)
            when(jnp.logical_and(within(i, 0, 4 * NCH - 1), kind_next), fetch, i + 1, down)
            now = jnp.logical_and(within(i, 0, 4 * NCH), kind)
            when(now, lambda down=down: wait((wbd if down else wbu).at[i % 2], w_sem.at[i % 2]))
        when(i == 2 * NCH, between_b)
        when(i == 3 * NCH, between_f)
        when(within(i, 2 * NCH, 3 * NCH), stage_e, i - 2 * NCH, False)
        when(within(i, 3 * NCH, 4 * NCH), stage_e, i - 2 * NCH, True)
        when(within(i, 0, NCH), stage_d, i, False, acc)
        when(within(i, NCH, 2 * NCH), stage_d, i, True, gh)
        when(within(i, 2 * NCH, NOUT), stage_d, i, False, acc)

        r = s - AT_H
        when(within(r, 0, NCH), stage_h_b, r)
        when(within(r, NCH, LAST), stage_h_f, r)
        when(r == LAST, stage_h_f, LAST, last_sum)
        when(r == NCH, finish_b)

        when(s == AT_C - 2, clear)
        when(s == AT_C - 1, load_cot)
        when(s == AT_C + 2, scale_tables)
        when(s == AT_C + 3, load_act)
        when(s == AT_C + 4, pick_tables, 0)
        when(within(s - (AT_C + 5), 0, SIDE), sum_tables, s - (AT_C + 5))
        return carry

    lax.fori_loop(0, AT_H + NRET, step, 0)

    def sent(n, carry):
        wait(ag.at[0, 0, pl.ds(0, 2)], a_s.at[n])
        wait(ag.at[0, :, pl.ds(0, 3), 0], b_s.at[n])

        def early():
            wait(ag.at[0, :, 3, 0], h_s.at[n])
            wait(ag.at[0, :, 3, 0], k_s.at[n])

        choose(n, early, lambda: wait(ag.at[0, :, 3], h_s.at[n]))
        return carry

    lax.fori_loop(1, NOUT, sent, 0)
    wait(ag.at[0, 0, 0], a_s.at[0])
    wait(ag.at[0, :, pl.ds(0, 3)], b_s.at[0])
    wait(far_tab, t_s.at[0])
    wait(tab.at[:, pl.ds(0, 3)], t_s.at[1])
    for n in range(NOUT - RING_S, NOUT):
        wait(snd.at[0], c_s.at[n])
    for r in range(NRET - RING_O, NRET):
        wait(ob.at[0, :, pl.ds(0, 3)], e_s.at[r])
    for r in range(NRET - RING_Z, LAST):
        if late(r):
            wait(zb.at[0, :, :, 3], v_s.at[r])
            wait(zb.at[0, :, 0, pl.ds(0, 3)], f_s.at[r])
        else:
            wait(zb.at[0, :, 0], f_s.at[r])
    wait(xl, f_s.at[LAST])
    for r in range(LAST - RING_X, LAST):
        wait(xb.at[0, :, pl.ds(0, 2)], g_s.at[r])
        if not late(r):
            wait(xb.at[0, :, 0], v_s.at[r])
    wait(xr.at[0, :, 0], g_s.at[LAST])
    wait(cot, p_s.at[0])
    wait(cot, p_s.at[1])
    wait(next_f, p_r.at[0])
    wait(next_b, p_r.at[1])


def per_device(
    act_fwd, routes_fwd, mix_fwd, cot_bwd, saved_bwd, routes_bwd, mix_bwd, norm_gain, w_up, w_down
):
    vmem, far = pl.BlockSpec(memory_space=pltpu.VMEM), pl.BlockSpec(memory_space=pl.ANY)
    sems = [pltpu.SemaphoreType.DMA((NOUT,))] * 6 + [pltpu.SemaphoreType.DMA((NRET,))] * 6
    sems += [pltpu.SemaphoreType.DMA((NOUT,))] * 4 + [pltpu.SemaphoreType.DMA((NRET,))] * 2
    sems += [pltpu.SemaphoreType.DMA((2,))] * 5
    out = jax.ShapeDtypeStruct((2, ROWS, D), BF)
    both = pl.pallas_call(
        kernel,
        out_shape=out,
        in_specs=[far, vmem, vmem, far, far, vmem, vmem, vmem, far, far],
        out_specs=far,
        scratch_shapes=[
            pltpu.VMEM((ROWS, D), BF),
            pltpu.VMEM((ROWS, D), BF),
            pltpu.VMEM((ROWS, D), BF),
            pltpu.SemaphoreType.DMA((3,)),
            pltpu.VMEM((2, SIDE - 1, DEEP, ROWS, CH), BF),
            pltpu.VMEM((NOUT, 2, SIDE, DEEP, ROWS, CH), BF),
            pltpu.VMEM((NOUT, 2, SIDE, SIDE, PAIR, CH), BF),
            pltpu.VMEM((RING_S, 2, SIDE - 1, SIDE, PAIR, CH), BF),
            pltpu.VMEM((2, 2, CH, HID), BF),
            pltpu.VMEM((2, 2, HID, CH), BF),
            pltpu.VMEM((RING_O, 2, SIDE, SIDE, PAIR, CH), BF),
            pltpu.VMEM((RING_Z, 2, DEEP, SIDE, ROWS, CH), BF),
            pltpu.VMEM((NRET, 2, SIDE, ROWS, CH), BF),
            pltpu.VMEM((RING_X, 2, SIDE, ROWS, CH), BF),
            pltpu.VMEM((NRET, 2, 2, ROWS, CH), BF),
            pltpu.VMEM((NCH, 2, ROWS, CH), F32),
            pltpu.VMEM((SIDE, LINE, HID), F32),
            pltpu.VMEM((SIDE, LINE, HID), F32),
            pltpu.VMEM((SIDE, LINE, HID), BF),
            pltpu.VMEM((2, 2, SIDE, LINE, PT), BF),
            pltpu.VMEM((2, SIDE, LINE, 128), F32),
            pltpu.VMEM((2, 2, SIDE, 2 * PT, LINE), BF),
            pltpu.VMEM((2, SIDE, 16, PT), F32),
            pltpu.VMEM((2, DEEP, SIDE, 16, PT), F32),
            pltpu.VMEM((2, SIDE, 16, PT), F32),
            pltpu.VMEM((2, SIDE, 16, PT), F32),
            pltpu.VMEM((NRET, 2, 2, DEEP, ROWS // 2, CH), BF),
        ]
        + sems,
        compiler_params=pltpu.CompilerParams(
            collective_id=0, has_side_effects=True, vmem_limit_bytes=63 * 2**20
        ),
        cost_estimate=pl.CostEstimate(flops=30 * 10**9, bytes_accessed=40 * 10**6, transcendentals=2 * 10**6),
    )(
        act_fwd[0], routes_fwd[0].T, mix_fwd[0].T, cot_bwd[0], saved_bwd[0], routes_bwd[0].T, mix_bwd[0].T,
        norm_gain, w_up[0, 0], w_down[0, 0],
    )
    return both[0:1], both[1:2]


def solution(mesh):
    rows = P("pipe", "expert", None)
    return jax.shard_map(
        per_device,
        mesh=mesh,
        in_specs=(rows,) * 7 + (P("pipe", None),) + (P("pipe", "expert", None, None),) * 2,
        out_specs=(rows, rows),
        check_vma=False,
    )
```

time: 231 us -> 225 us (0.974)
  Pallas kernels: 224 us -> 219 us
    pallas_call x1, Pallas kernels: 224 us -> 219 us  [per_device(): pl.pallas_call(kernel, out_shape=out, in_specs=[far, vmem, vmem, far, far...]
    unnamed x2 -> x0, local copies, waits for them, and re-layouts: 3.63 us -> none
where the time goes in v3:
time: 225 us; the launch traced here: 221 us
  Pallas kernels  219 us (97%)
    pallas_call x1, Pallas kernels, per_device(): pl.pallas_call(kernel, out_shape=out, in_specs=[far, vmem, vmem, far, far...  219 us

profile of v3, /device:TPU:6, one launch (start us, length us, event | category | flops | bytes accessed | tf_op | source)
XLA Modules:
  0.0 221.4 jit_solution(12424890152890851666)
XLA Ops:
  0.6 218.6 %shard_map.113 = bf16[2,64,3584]{2,1,0:T(8,128)(2,1)} custom-call(bf16[64,3584]{1,0:T(8,128)(2,1)} %bitcast.19, s32[8,64]{1,0:T(8,128)} %bitcast.22, f32[8,64]{1,0:T(8,128)} %bitcast.23, bf16[64,3584]{1,0:T(8,128)(2,1)} %bitcast.20, bf16[64,3584]{1,0:T(8,128)(2,1)} %bitcast.21, s32[8,64]{1,0:T(8,128)} %bitcast.24, f32[8,64]{1,0:T(8,128)} %bitcast.25, ...), custom_call_target="tpu_custom_call" | custom-call | flops 30000001024 | bytes 40000000 | tf_op jit(solution)/shard_map/pallas_call | solution.py:590
  219.2 2.1 fusion

commit v4 on v3

--- a/solution.py
+++ b/solution.py
@@ -21,14 +21,20 @@
 NOUT, NRET = 3 * NCH, 2 * NCH
 RING_S, RING_O, RING_Z, RING_X = 3, 4, 7, 5
 LAST = NRET - 1
-AT_A, AT_B, AT_W, AT_C, AT_D = 0, 2, 3, 6, 7
+AT_A, AT_B, AT_W, AT_C, AT_D = 0, 6, 7, 8, 11
 AT_E = AT_D + 2 * NCH
-AT_F, AT_G, AT_V, AT_H = AT_E + 2, AT_E + 5, AT_E + 7, AT_E + 11
+AT_F, AT_G, AT_V, AT_H = AT_E + 4, AT_E + 7, AT_E + 10, AT_E + 13
 SLOT = {0: 1, 1: 2, 2: 3, 3: 0}
 
 
-def late(n):
-    return n < 0
+LATE_OUT, LATE_BACK = (1, 2, 10, 11, 12, 13, 15, 16), (5, 8, 11)
+
+
+def among(n, chunks):
+    found = n == chunks[0]
+    for one in chunks[1:]:
+        found = jnp.logical_or(found, n == one)
+    return found
 
 
 def kernel(
@@ -62,7 +68,8 @@
         pltpu.make_async_copy(ref, ref, sem).wait()
 
     barrier = pltpu.get_barrier_semaphore()
-    peers = [other, ahead, behind] + [gather_peer(v, k) for v in range(2) for k in shifts]
+    other_ahead, other_behind = (ahead[0], other[1]), (behind[0], other[1])
+    peers = [other, ahead, behind, other_behind] + [gather_peer(v, k) for v in range(2) for k in shifts]
     for peer in peers:
         pl.semaphore_signal(barrier, inc=1, device_id=peer, device_id_type=MESH)
 
@@ -105,9 +112,11 @@
     loads[0].wait()
     spread(0, normed(saved)[0] * gain[...])
 
-    def choose(n, early, after):
-        pl.when(late(n))(after)
-        pl.when(jnp.logical_not(late(n)))(early)
+    def choose(late, early, after):
+        pl.when(late)(after)
+        pl.when(jnp.logical_not(late))(early)
+
+    late_out, late_back = (lambda n: among(n, LATE_OUT)), (lambda r: among(r, LATE_BACK))
 
     top, bottom = pl.ds(0, ROWS // 2), pl.ds(ROWS // 2, ROWS // 2)
 
@@ -123,7 +132,7 @@
             part = ag.at[n, v, pl.ds(0, 3), z]
             send(part, part, b_s.at[n], b_r.at[n], other)
 
-        @pl.when(jnp.logical_not(late(n)))
+        @pl.when(jnp.logical_not(late_out(n)))
         def _():
             for v in range(2):
                 send(ag.at[n, v, 0, z, top], ag.at[n, v, 3, z, top], h_s.at[n], h_r.at[n], gather_peer(v, 1))
@@ -141,14 +150,14 @@
                 send(ag.at[n, v, 0, :, top], ag.at[n, v, 3, :, top], h_s.at[n], h_r.at[n], gather_peer(v, 1))
                 send(ag.at[n, v, 2, :, bottom], ag.at[n, v, 3, :, bottom], h_s.at[n], h_r.at[n], gather_peer(v, 3))
 
-        choose(n, early, after)
+        choose(late_out(n), early, after)
 
     def gathered(n):
         def early():
             wait(ag.at[n, :, pl.ds(0, 3), 0], b_r.at[n])
             wait(ag.at[n, :, 3, 0], k_r.at[n])
 
-        choose(n, early, lambda: wait(ag.at[n, :, 3], h_r.at[n]))
+        choose(late_out(n), early, lambda: wait(ag.at[n, :, 3], h_r.at[n]))
 
     def first_a():
         for v in range(2):
@@ -277,7 +286,7 @@
             wait(zb.at[0, :, :, 3], v_s.at[r])
             wait(zb.at[0, :, 0, pl.ds(0, 3)], f_s.at[r])
 
-        choose(r, early, after)
+        choose(late_back(r), early, after)
 
     def stage_f(r):
         combine(r)
@@ -292,7 +301,7 @@
                 send(zb.at[ring, v, :, 3, top], xf.at[r, v, 0], v_s.at[r], v_r.at[r], gather_peer(v, 1))
                 send(zb.at[ring, v, :, 3, bottom], xf.at[r, v, 1], v_s.at[r], v_r.at[r], gather_peer(v, 3))
 
-        choose(r, early, after)
+        choose(late_back(r), early, after)
 
     def stage_g(r):
         ring, xring = r % RING_Z, r % RING_X
@@ -300,7 +309,7 @@
         @pl.when(r >= RING_X)
         def _():
             wait(xb.at[0, :, pl.ds(0, 2)], g_s.at[r - RING_X])
-            pl.when(jnp.logical_not(late(r - RING_X)))(lambda: wait(xb.at[0, :, 0], v_s.at[r - RING_X]))
+            pl.when(jnp.logical_not(late_back(r - RING_X)))(lambda: wait(xb.at[0, :, 0], v_s.at[r - RING_X]))
 
         def early():
             wait(zr.at[r], f_r.at[r])
@@ -318,16 +327,16 @@
                 part = pl.ds(0, 3)
                 send(zb.at[ring, v, 1 - z, part], zr.at[r, v, part], f_s.at[r], f_r.at[r], other)
 
-        choose(r, early, after)
+        choose(late_back(r), early, after)
 
     def stage_v(r):
         ring, xring = r % RING_Z, r % RING_X
-        choose(r, lambda: wait(xf.at[r, :, :, 0], v_r.at[r]), lambda: wait(zr.at[r, :, pl.ds(0, 3)], f_r.at[r]))
+        choose(late_back(r), lambda: wait(xf.at[r, :, :, 0], v_r.at[r]), lambda: wait(zr.at[r, :, pl.ds(0, 3)], f_r.at[r]))
         for v in range(2):
             for i in range(3):
                 xb[xring, v, i] = (zb[ring, v, z, i].astype(F32) + zr[r, v, i].astype(F32)).astype(BF)
 
-            @pl.when(jnp.logical_not(late(r)))
+            @pl.when(jnp.logical_not(late_back(r)))
             def _():
                 for i, rows, j in ((2, top, 0), (0, bottom, 1)):
                     xb[xring, v, i, rows] = (
@@ -337,8 +346,8 @@
             send(xb.at[xring, v, 2], xr.at[r, v, 0], g_s.at[r], g_r.at[r], gather_peer(v, 1))
             send(xb.at[xring, v, 0], xr.at[r, v, 1], g_s.at[r], g_r.at[r], gather_peer(v, 3))
 
-    xz = wbu.at[0]
     half = lambda zz: pl.ds(pl.multiple_of(zz * ROWS, ROWS), ROWS)
+    at_last = lambda v: pl.ds(v * HALF + (LAST - NCH) * CH, CH)
 
     def last_f():
         combine(LAST)
@@ -354,8 +363,25 @@
                 out = zb[LAST % RING_Z, v, zz, 1].astype(F32)
                 for k in range(SIDE - 1):
                     out = out + xl[v, k, zz].astype(F32)
-                xz[v, zz * ROWS : (zz + 1) * ROWS, :CH] = out.astype(BF)
-            send(xz.at[v, half(1 - z), pl.ds(0, CH)], xr.at[LAST, v, 0], g_s.at[LAST], g_r.at[LAST], other)
+                acc[zz, :ROWS, :CH] = out
+                wbu[0, v, zz * ROWS : (zz + 1) * ROWS, :CH] = out.astype(BF)
+            send(wbu.at[0, v, half(1 - z), pl.ds(0, CH)], xr.at[LAST, v, 0], g_s.at[LAST], g_r.at[LAST], other_ahead)
+            own = act[:, at_last(v)].astype(F32) + acc[z, :ROWS, :CH]
+            high = own.astype(BF)
+            wbu[0, v, :ROWS, CH : 2 * CH] = high
+            wbu[0, v, :ROWS, 2 * CH : 3 * CH] = (own - high.astype(F32)).astype(BF)
+            for part in range(2):
+                for h, rows in enumerate((top, bottom)):
+                    src = wbu.at[0, v, rows, pl.ds((part + 1) * CH, CH)]
+                    send(src, xf.at[LAST, v, part, h], v_s.at[LAST], v_r.at[LAST], ahead)
+
+    def last_h():
+        wait(xr.at[LAST, :, 0], g_r.at[LAST])
+        wait(xf.at[LAST], v_r.at[LAST])
+        for v in range(2):
+            own = (xf[LAST, v, 0].astype(F32) + xf[LAST, v, 1].astype(F32)).reshape(ROWS, CH)
+            wbu[1, v, :ROWS, :CH] = (own + xr[LAST, v, 0].astype(F32)).astype(BF)
+            pltpu.make_async_copy(wbu.at[1, v, pl.ds(0, ROWS), pl.ds(0, CH)], next_f.at[:, at_last(v)], i_s.at[v]).start()
 
     def summed(r, v):
         return xb[r % RING_X, v, 1].astype(F32) + xr[r, v, 0].astype(F32) + xr[r, v, 1].astype(F32)
@@ -365,18 +391,12 @@
         for v in range(2):
             gs[r, v] = summed(r, v)
 
-    def last_sum(r, v):
-        return xz[v, half(z), :CH].astype(F32) + xr[LAST, v, 0].astype(F32)
-
-    def stage_h_f(r, total=summed):
-        if total is summed:
-            wait(xr.at[r], g_r.at[r])
-        else:
-            wait(xr.at[LAST, :, 0], g_r.at[LAST])
+    def stage_h_f(r):
+        wait(xr.at[r], g_r.at[r])
         j = r - NCH
         for v in range(2):
             cols = pl.ds(pl.multiple_of(v * HALF + j * CH, CH), CH)
-            act[:, cols] = (act[:, cols].astype(F32) + total(r, v)).astype(BF)
+            act[:, cols] = (act[:, cols].astype(F32) + summed(r, v)).astype(BF)
             send(act.at[:, cols], next_f.at[:, cols], p_s.at[0], p_r.at[0], ahead)
 
     def finish_b():
@@ -499,6 +519,8 @@
         when(within(s - AT_F, 0, LAST), stage_f, s - AT_F)
         when(s - AT_F == LAST, last_f)
         when(within(s - AT_W, 1, NOUT), stage_w, s - AT_W)
+        when(s - AT_A == NCH, load_cot)
+        when(s - AT_A == 2 * NCH, load_act)
         when(within(s - AT_A, 2, NOUT), stage_a, s - AT_A)
         when(within(s - AT_V, 0, LAST), stage_v, s - AT_V)
         when(within(s - AT_G, 0, LAST), stage_g, s - AT_G)
@@ -528,13 +550,11 @@
         r = s - AT_H
         when(within(r, 0, NCH), stage_h_b, r)
         when(within(r, NCH, LAST), stage_h_f, r)
-        when(r == LAST, stage_h_f, LAST, last_sum)
+        when(r == LAST, last_h)
         when(r == NCH, finish_b)
 
-        when(s == AT_C - 2, clear)
-        when(s == AT_C - 1, load_cot)
+        when(s == AT_C - 1, clear)
         when(s == AT_C + 2, scale_tables)
-        when(s == AT_C + 3, load_act)
         when(s == AT_C + 4, pick_tables, 0)
         when(within(s - (AT_C + 5), 0, SIDE), sum_tables, s - (AT_C + 5))
         return carry
@@ -549,7 +569,7 @@
             wait(ag.at[0, :, 3, 0], h_s.at[n])
             wait(ag.at[0, :, 3, 0], k_s.at[n])
 
-        choose(n, early, lambda: wait(ag.at[0, :, 3], h_s.at[n]))
+        choose(late_out(n), early, lambda: wait(ag.at[0, :, 3], h_s.at[n]))
         return carry
 
     lax.fori_loop(1, NOUT, sent, 0)
@@ -562,7 +582,7 @@
     for r in range(NRET - RING_O, NRET):
         wait(ob.at[0, :, pl.ds(0, 3)], e_s.at[r])
     for r in range(NRET - RING_Z, LAST):
-        if late(r):
+        if r in LATE_BACK:
             wait(zb.at[0, :, :, 3], v_s.at[r])
             wait(zb.at[0, :, 0, pl.ds(0, 3)], f_s.at[r])
         else:
@@ -570,13 +590,17 @@
     wait(xl, f_s.at[LAST])
     for r in range(LAST - RING_X, LAST):
         wait(xb.at[0, :, pl.ds(0, 2)], g_s.at[r])
-        if not late(r):
+        if r not in LATE_BACK:
             wait(xb.at[0, :, 0], v_s.at[r])
     wait(xr.at[0, :, 0], g_s.at[LAST])
-    wait(cot, p_s.at[0])
+    wait(xf.at[LAST], v_s.at[LAST])
+    most = pl.ds(0, D - 2 * CH)
+    wait(cot.at[:, most], p_s.at[0])
     wait(cot, p_s.at[1])
-    wait(next_f, p_r.at[0])
+    wait(next_f.at[:, most], p_r.at[0])
     wait(next_b, p_r.at[1])
+    for v in range(2):
+        wait(next_f.at[:, at_last(v)], i_s.at[v])
 
 
 def per_device(

time: 225 us -> 221 us (0.982)
  no operation moved by 1% of the time
where the time goes in v4:
time: 221 us; the launch traced here: 220 us
  Pallas kernels  217 us (98%)
    pallas_call x1, Pallas kernels, per_device(): pl.pallas_call(kernel, out_shape=out, in_specs=[far, vmem, vmem, far, far...  217 us

profile of v4, /device:TPU:6, one launch (start us, length us, event | category | flops | bytes accessed | tf_op | source)
XLA Modules:
  0.0 219.6 jit_solution(643572725579410684)
XLA Ops:
  0.6 216.8 %shard_map.113 = bf16[2,64,3584]{2,1,0:T(8,128)(2,1)} custom-call(bf16[64,3584]{1,0:T(8,128)(2,1)} %bitcast.19, s32[8,64]{1,0:T(8,128)} %bitcast.22, f32[8,64]{1,0:T(8,128)} %bitcast.23, bf16[64,3584]{1,0:T(8,128)(2,1)} %bitcast.20, bf16[64,3584]{1,0:T(8,128)(2,1)} %bitcast.21, s32[8,64]{1,0:T(8,128)} %bitcast.24, f32[8,64]{1,0:T(8,128)} %bitcast.25, ...), custom_call_target="tpu_custom_call" | custom-call | flops 30000001024 | bytes 40000000 | tf_op jit(solution)/shard_map/pallas_call | solution.py:614
  217.4 2.1 fusion

commit v5 on v4

--- a/solution.py
+++ b/solution.py
@@ -38,9 +38,9 @@
 
 
 def kernel(
-    act_far, routes_f, mix_f, cot_far, saved_far, routes_b, mix_b, gain, wup, wdn,
+    act_far, routes_f_far, mix_f_far, cot_far, saved_far, routes_b_far, mix_b_far, gain_far, wup, wdn,
     both_next,
-    act, cot, saved, i_s, xl,
+    act, cot, saved, routes_f, mix_f, routes_b, mix_b, gain, i_s, xl,
     ag, rc, snd, wbu, wbd, ob, zb, zr, xb, xr, gs, acc, gh, hid, sel, scl, cw, tab, own_tab, far_tab, pair_tab, xf,
     a_s, a_r, b_s, b_r, c_s, c_r, e_s, e_r, f_s, f_r, g_s, g_r, h_s, h_r, k_s, k_r, v_s, v_r, w_sem, t_s, t_r, p_s, p_r,
 ):
@@ -73,9 +73,13 @@
     for peer in peers:
         pl.semaphore_signal(barrier, inc=1, device_id=peer, device_id_type=MESH)
 
-    loads = [pltpu.make_async_copy(far, near, i_s.at[i]) for i, (far, near) in enumerate(((saved_far, saved), (cot_far, cot), (act_far, act)))]
-    for load in loads:
+    pairs = (saved_far, saved), (cot_far, cot), (act_far, act), (gain_far, gain)
+    pairs += (routes_f_far, routes_f), (mix_f_far, mix_f), (routes_b_far, routes_b), (mix_b_far, mix_b)
+    loads = [pltpu.make_async_copy(far, near, i_s.at[i]) for i, (far, near) in enumerate(pairs)]
+    for load in loads[3:] + loads[:3]:
         load.start()
+    for load in loads[3:]:
+        load.wait()
 
     line = lax.broadcasted_iota(jnp.int32, (128, PT), 0)
     mine = lax.broadcasted_iota(jnp.int32, (128, PT), 1) // ROWS == z
@@ -606,7 +610,7 @@
 def per_device(
     act_fwd, routes_fwd, mix_fwd, cot_bwd, saved_bwd, routes_bwd, mix_bwd, norm_gain, w_up, w_down
 ):
-    vmem, far = pl.BlockSpec(memory_space=pltpu.VMEM), pl.BlockSpec(memory_space=pl.ANY)
+    far = pl.BlockSpec(memory_space=pl.ANY)
     sems = [pltpu.SemaphoreType.DMA((NOUT,))] * 6 + [pltpu.SemaphoreType.DMA((NRET,))] * 6
     sems += [pltpu.SemaphoreType.DMA((NOUT,))] * 4 + [pltpu.SemaphoreType.DMA((NRET,))] * 2
     sems += [pltpu.SemaphoreType.DMA((2,))] * 5
@@ -614,13 +618,18 @@
     both = pl.pallas_call(
         kernel,
         out_shape=out,
-        in_specs=[far, vmem, vmem, far, far, vmem, vmem, vmem, far, far],
+        in_specs=[far] * 10,
         out_specs=far,
         scratch_shapes=[
             pltpu.VMEM((ROWS, D), BF),
             pltpu.VMEM((ROWS, D), BF),
             pltpu.VMEM((ROWS, D), BF),
-            pltpu.SemaphoreType.DMA((3,)),
+            pltpu.VMEM((TOP, ROWS), jnp.int32),
+            pltpu.VMEM((TOP, ROWS), F32),
+            pltpu.VMEM((TOP, ROWS), jnp.int32),
+            pltpu.VMEM((TOP, ROWS), F32),
+            pltpu.VMEM((1, D), F32),
+            pltpu.SemaphoreType.DMA((8,)),
             pltpu.VMEM((2, SIDE - 1, DEEP, ROWS, CH), BF),
             pltpu.VMEM((NOUT, 2, SIDE, DEEP, ROWS, CH), BF),
             pltpu.VMEM((NOUT, 2, SIDE, SIDE, PAIR, CH), BF),

time: 221 us -> 221 us (level)
  no operation moved by 1% of the time
where the time goes in v5:
time: 221 us; the launch traced here: 219 us
  Pallas kernels  217 us (98%)
    pallas_call x1, Pallas kernels, per_device(): pl.pallas_call(kernel, out_shape=out, in_specs=[far] * 10, out_specs=far,...  217 us

profile of v5, /device:TPU:6, one launch (start us, length us, event | category | flops | bytes accessed | tf_op | source)
XLA Modules:
  0.0 219.3 jit_solution(980597821612895807)
XLA Ops:
  0.6 216.6 %shard_map.113 = bf16[2,64,3584]{2,1,0:T(8,128)(2,1)} custom-call(bf16[64,3584]{1,0:T(8,128)(2,1)} %bitcast.19, s32[8,64]{1,0:T(8,128)} %bitcast.22, f32[8,64]{1,0:T(8,128)} %bitcast.23, bf16[64,3584]{1,0:T(8,128)(2,1)} %bitcast.20, bf16[64,3584]{1,0:T(8,128)(2,1)} %bitcast.21, s32[8,64]{1,0:T(8,128)} %bitcast.24, f32[8,64]{1,0:T(8,128)} %bitcast.25, ...), custom_call_target="tpu_custom_call" | custom-call | flops 30000001024 | bytes 40000000 | tf_op jit(solution)/shard_map/pallas_call | solution.py:618
  217.2 2.1 fusion
